TPU v7x, 128 devices: a whole 4x4x4 slice. The times are simulated.
128 devices in a mesh: band: 32 (over y_hi, x, z), grid: 4 (over y_lo, core).
Axes of the slice: x: 4, y: 4 (y_hi: 2, y_lo: 2; y = y_hi * 2 + y_lo), z: 4, core: 2. Of those that a mesh axis runs over, the one named last changes fastest.
Arguments:
- orbitals: float32 [64, 128, 16384], P('band', 'grid'), may hold values from -6 to 6
- occupation: float32 [64], P('band'), may hold values from 0.1 to 1
- pair_keep: int32 [64, 2, 2], P('band'), may hold values 0 or 1
Outputs:
- exchange_term: float32 [64, 128, 16384], P('band', 'grid')
All inputs are finite; a program needn't handle non-finite values. No bound on the sum of `pair_keep` on one device may be relied on, other than what follows from the above.
Results may differ from a plain program's by a relative error of at most 0.0065.
Values may be sent and summed in bfloat16 or wider, within the bound.
A program may use at most 128 MiB of HBM per device.

v0:
```python
import math

import jax
import jax.numpy as jnp
from jax import lax
from jax.sharding import PartitionSpec as P

GRID = 128


screen_width = 64.0


def shifted(value, axis, steps):
    count = lax.axis_size(axis)
    pairs = [(source, (source + steps) % count) for source in range(count)]
    return lax.ppermute(value, axis, pairs)


def make_tables():
    wave_index = jnp.arange(GRID, dtype=jnp.int32)
    phase_angle = (wave_index[:, None] * wave_index[None, :] % GRID).astype(jnp.float32) * (
        2.0 * math.pi / GRID
    )
    cosine = jnp.cos(phase_angle)
    sine_part = jnp.sin(phase_angle)
    result_tables = []
    for direction_sign in (1.0, -1.0):
        signed_sine = sine_part * direction_sign
        line_table = jnp.concatenate([cosine, signed_sine], axis=1).astype(jnp.bfloat16)
        square_table = jnp.concatenate(
            [
                jnp.concatenate([cosine, -signed_sine], axis=1),
                jnp.concatenate([signed_sine, cosine], axis=1),
            ],
            axis=0,
        ).astype(jnp.bfloat16)
        result_tables.append((line_table, square_table))
    return result_tables


def signed_freq(indices):
    return jnp.where(indices >= GRID // 2, indices - GRID, indices).astype(jnp.float32)


def coulomb_kernel(rows_x, rows_y):
    depth_index = jnp.arange(2 * GRID, dtype=jnp.int32) % GRID
    squared = (
        signed_freq(rows_x)[:, None, None] ** 2
        + signed_freq(rows_y)[None, :, None] ** 2
        + signed_freq(depth_index)[None, None, :] ** 2
    )
    scaled_q = squared / screen_width
    safe_q = jnp.where(scaled_q > 0, scaled_q, 1.0)
    ratio = jnp.where(scaled_q > 0, -jnp.expm1(-scaled_q) / safe_q, 1.0)
    return ratio * (4.0 / GRID**3)


def rotated(values):
    half_width = values.shape[-1] // 2
    return jnp.concatenate([values[..., half_width:], -values[..., :half_width]], axis=-1)


def along_y(table, values):
    stacked = jnp.concatenate([values, rotated(values)], axis=2)
    return jnp.einsum("vy,nxyk->nxvk", table, stacked, preferred_element_type=jnp.float32)


def along_x(table, values):
    stacked = jnp.concatenate([values, rotated(values)], axis=1)
    return jnp.einsum("vx,nxyk->nvyk", table, stacked, preferred_element_type=jnp.float32)


def pair_terms(own_bands, own_occ, visit_pairs, visit_occ, keep_rows, tables, kernel):
    group = own_bands.shape[0]
    halves = visit_pairs.shape[0]
    plane_rows = own_bands.shape[1]
    forward_tables, inverse_tables = tables
    own_grid = own_bands.reshape(group, plane_rows, GRID, GRID)
    own_twice = jnp.concatenate([own_grid, own_grid], axis=-1)
    density = (
        (own_twice[:, None] * visit_pairs[None])
        .reshape(group * halves, plane_rows, GRID, 2 * GRID)
        .astype(jnp.bfloat16)
    )
    spectrum = jnp.dot(density, forward_tables[1], preferred_element_type=jnp.float32).astype(
        jnp.bfloat16
    )
    spectrum = along_y(forward_tables[0], spectrum).astype(jnp.bfloat16)
    screened = (
        along_x(
            forward_tables[0],
            lax.all_to_all(spectrum, "grid", split_axis=2, concat_axis=1, tiled=True),
        )
        * kernel
    ).astype(jnp.bfloat16)
    back_lines = along_x(inverse_tables[0], screened).astype(jnp.bfloat16)
    spectrum = lax.all_to_all(back_lines, "grid", split_axis=1, concat_axis=2, tiled=True)
    spectrum = along_y(inverse_tables[0], spectrum).astype(jnp.bfloat16)
    potential = jnp.dot(spectrum, inverse_tables[1], preferred_element_type=jnp.float32)
    potential = potential.reshape(group, halves, plane_rows, GRID, 2 * GRID)
    keep_float = keep_rows.astype(jnp.float32)
    weight_own = jnp.repeat(
        (visit_occ[None, :] * keep_float).reshape(group, halves, 2), GRID, axis=-1
    )
    weight_partner = jnp.repeat(
        (own_occ[:, None] * keep_float).reshape(group, halves, 2), GRID, axis=-1
    )
    own_sum = jnp.sum(weight_own[:, :, None, None, :] * potential * visit_pairs[None], axis=1)
    own_part = (own_sum[..., :GRID] + own_sum[..., GRID:]).reshape(group, plane_rows, GRID * GRID)
    partner_sum = jnp.sum(
        weight_partner[:, :, None, None, :] * potential * own_twice[:, None], axis=0
    )
    partner_part = (
        partner_sum.reshape(halves, plane_rows, GRID, 2, GRID)
        .transpose(0, 3, 1, 2, 4)
        .reshape(2 * halves, plane_rows, GRID * GRID)
    )
    return (own_part, partner_part)


def block_step(orbitals, occupation, keep_step, visitors, visitor_occ, tables, kernel):
    band_count, plane_rows, cell_count = orbitals.shape
    halves = band_count // 2
    visit_pairs = (
        visitors.reshape(halves, 2, plane_rows, GRID, GRID)
        .transpose(0, 2, 3, 1, 4)
        .reshape(halves, plane_rows, GRID, 2 * GRID)
    )

    def one_group(partner_total, inputs):
        own_bands, own_occ, keep_rows = inputs
        own_part, partner_part = pair_terms(
            own_bands, own_occ, visit_pairs, visitor_occ, keep_rows, tables, kernel
        )
        return (partner_total + partner_part, own_part)

    partner_total, own_parts = lax.scan(
        one_group,
        jnp.zeros((band_count, plane_rows, cell_count), jnp.float32),
        (
            orbitals.reshape(halves, 2, plane_rows, cell_count),
            occupation.reshape(halves, 2),
            keep_step.reshape(halves, 2, band_count),
        ),
    )
    return (own_parts.reshape(band_count, plane_rows, cell_count), partner_total)


def body(orbitals, occupation, pair_keep):
    tables = make_tables()
    line_width = GRID // lax.axis_size("grid")
    column_index = lax.axis_index("grid") * line_width + jnp.arange(line_width, dtype=jnp.int32)
    kernel = coulomb_kernel(jnp.arange(GRID, dtype=jnp.int32), column_index)
    near_bands, near_occ = shifted((orbitals, occupation), "band", 1)
    near_own, near_partner = block_step(
        orbitals, occupation, pair_keep[:, 0, :], near_bands, near_occ, tables, kernel
    )
    far_bands, far_occ, carried = shifted((near_bands, near_occ, near_partner), "band", 1)
    far_own, far_partner = block_step(
        orbitals, occupation, pair_keep[:, 1, :], far_bands, far_occ, tables, kernel
    )
    returned = shifted((carried + far_partner).astype(jnp.bfloat16), "band", -2).astype(jnp.float32)
    return -(near_own + far_own + returned)


def solution(mesh):
    in_specs = (P("band", "grid", None), P("band"), P("band", None, None))
    out_specs = P("band", "grid", None)
    return jax.shard_map(body, mesh=mesh, in_specs=in_specs, out_specs=out_specs, check_vma=False)
```

profile of v0, /device:TPU:2, one launch (start us, length us, event | category | flops | bytes accessed | tf_op | source)
XLA Modules:
  0.0 604.2 jit_solution(10082474286326197774)
XLA Ops:
  1.9 93.0 %collective-permute-done.1 = f32[2,32,16384]{2,1,0:T(8,128)} collective-permute-done((f32[2,32,16384]{2,1,0:T(8,128)}, f32[2,32,16384]{2,1,0:T(8,128)}, u32[]{:S(2)}, u32[]{:S(2)}) %collective-permute-start.1) | collective-permute-done | bytes 4194336 | tf_op jit(solution)/shard_map/ppermute | solution.py:17
  99.2 6.0 copy.104
  110.5 6.4 %mul.313 = f32[32,128,256]{2,1,0:T(8,128)} reshape(f32[1,32,128,2,128]{4,3,2,1,0:T(2,128)} %copy.56) | data formatting | bytes 8388608 | tf_op jit(solution)/shard_map/while/body/eval_jaxpr/mul | solution.py:82
  127.3 8.0 %copy.58 = bf16[2,32,128,256]{3,1,0,2:T(8,128)(2,1)} copy(bf16[2,32,128,256]{2,3,1,0:T(8,128)(2,1)} %convert_bitcast_fusion.3) | data formatting | bytes 8388608 | tf_op jit(solution)/shard_map/while/body/eval_jaxpr/convert_element_type | solution.py:89
  140.6 48.3 %collective-permute-done.3 = f32[2,32,16384]{2,1,0:T(8,128)} collective-permute-done((f32[2,32,16384]{2,1,0:T(8,128)}, f32[2,32,16384]{2,1,0:T(8,128)}, u32[]{:S(2)}, u32[]{:S(2)}) %collective-permute-start.3) | collective-permute-done | bytes 4194336 | tf_op jit(solution)/shard_map/ppermute | solution.py:17
  197.2 6.4 %mul.333 = f32[32,128,256]{2,1,0:T(8,128)} reshape(f32[1,32,128,2,128]{4,3,2,1,0:T(2,128)} %copy.71) | data formatting | bytes 8388608 | tf_op jit(solution)/shard_map/while/body/eval_jaxpr/mul | solution.py:82
  203.6 5.8 fusion.75
  214.0 8.0 %copy.73 = bf16[2,32,128,256]{3,1,0,2:T(8,128)(2,1)} copy(bf16[2,32,128,256]{2,3,1,0:T(8,128)(2,1)} %convert_bitcast_fusion.1) | data formatting | bytes 8388608 | tf_op jit(solution)/shard_map/while/body/eval_jaxpr/convert_element_type | solution.py:89
  231.6 6.8 %copy.60 = bf16[2,4,32,32,256]{4,3,2,1,0:T(8,128)(2,1)} copy(bf16[2,4,32,32,256]{4,2,0,3,1:T(8,128)(2,1)} %bitcast.9) | data formatting | bytes 8388608 | tf_op jit(solution)/shard_map/while/body/eval_jaxpr/all_to_all | solution.py:93
  238.4 7.9 %copy.63 = bf16[2,128,32,256]{1,3,2,0:T(8,128)(2,1)} copy(bf16[2,128,32,256]{3,2,1,0:T(8,128)(2,1)} %bitcast.131) | data formatting | bytes 8388608 | tf_op jit(solution)/shard_map/while/body/eval_jaxpr/all_to_all | solution.py:93
  258.2 7.9 %copy.64 = bf16[2,128,32,256]{3,2,0,1:T(8,128)(2,1)} copy(bf16[2,128,32,256]{1,3,2,0:T(8,128)(2,1)} %convert_bitcast_fusion.2) | data formatting | bytes 8388608 | tf_op jit(solution)/shard_map/while/body/eval_jaxpr/convert_element_type | solution.py:97
  266.1 9.1 %all-to-all-done.2 = bf16[2,32,128,256]{3,1,0,2:T(8,128)(2,1)} async-done(((bf16[2,32,128,256]{3,1,0,2:T(8,128)(2,1)}), bf16[2,32,128,256]{3,1,0,2:T(8,128)(2,1)}, u32[]{:S(2)}, u32[]{:S(2)}) %all-to-all-start.2) | async-done | bytes 4194336 | tf_op jit(solution)/shard_map/while/body/eval_jaxpr/all_to_all | solution.py:93
  280.4 6.8 %copy.75 = bf16[2,4,32,32,256]{4,3,2,1,0:T(8,128)(2,1)} copy(bf16[2,4,32,32,256]{4,2,0,3,1:T(8,128)(2,1)} %bitcast.29) | data formatting | bytes 8388608 | tf_op jit(solution)/shard_map/while/body/eval_jaxpr/all_to_all | solution.py:93
  287.2 8.0 %copy.78 = bf16[2,128,32,256]{1,3,2,0:T(8,128)(2,1)} copy(bf16[2,128,32,256]{3,2,1,0:T(8,128)(2,1)} %bitcast.132) | data formatting | bytes 8388608 | tf_op jit(solution)/shard_map/while/body/eval_jaxpr/all_to_all | solution.py:93
  307.0 8.0 %copy.79 = bf16[2,128,32,256]{3,2,0,1:T(8,128)(2,1)} copy(bf16[2,128,32,256]{1,3,2,0:T(8,128)(2,1)} %convert_bitcast_fusion) | data formatting | bytes 8388608 | tf_op jit(solution)/shard_map/while/body/eval_jaxpr/convert_element_type | solution.py:97
  315.0 13.6 %all-to-all-done.1 = bf16[2,128,32,256]{3,2,0,1:T(8,128)(2,1)} async-done(((bf16[2,128,32,256]{3,2,0,1:T(8,128)(2,1)}), bf16[2,128,32,256]{3,2,0,1:T(8,128)(2,1)}, u32[]{:S(2)}, u32[]{:S(2)}) %all-to-all-start.1) | async-done | bytes 4194336 | tf_op jit(solution)/shard_map/while/body/eval_jaxpr/all_to_all | solution.py:98
  333.6 21.2 %collective-permute-done = f32[2]{0:T(128)S(1)} collective-permute-done((f32[2]{0:T(128)S(1)}, f32[2]{0:T(128)S(1)}, u32[]{:S(2)}, u32[]{:S(2)}) %collective-permute-start) | collective-permute-done | bytes 40 | tf_op jit(solution)/shard_map/ppermute | solution.py:17
  366.0 6.4 %copy.69 = bf16[2,32,128,256]{2,3,1,0:T(8,128)(2,1)} copy(bf16[2,32,128,256]{3,2,1,0:T(8,128)(2,1)} %bitcast.133) | data formatting | bytes 8388608 | tf_op jit(solution)/shard_map/while/body/eval_jaxpr/all_to_all | solution.py:98
  376.3 8.5 %fusion.57 = f32[2,32,128,256]{3,2,1,0:T(8,128)} fusion(bf16[2,32,128,128]{2,3,1,0:T(8,128)(2,1)} %get-tuple-element.60, bf16[2,32,128,128]{2,3,1,0:T(8,128)(2,1)S(1)} %get-tuple-element.59, bf16[2,32,128,256]{2,3,1,0:T(8,128)(2,1)} %copy.69, bf16[128,128]{1,0:T(8,128)(2,1)S(1)} %get-tuple-element.116, bf16[128,128]{1,0:T(8,128)(2,1)S(1)} %get-tuple-element.118, ...), kind=kOutput, calls=%fused_computation.71 | convolution fusion | flops 2175401984 | bytes 16875520 | tf_op jit(solution)/shard_map/while/body/eval_jaxpr/dot_general | solution.py:100
  389.6 6.4 %copy.84 = bf16[2,32,128,256]{2,3,1,0:T(8,128)(2,1)} copy(bf16[2,32,128,256]{3,2,1,0:T(8,128)(2,1)} %bitcast.134) | data formatting | bytes 8388608 | tf_op jit(solution)/shard_map/while/body/eval_jaxpr/all_to_all | solution.py:98
  400.0 22.9 %multiply_reduce_fusion = (f32[32,128,256]{2,1,0:T(8,128)}, f32[32,128,256]{2,1,0:T(8,128)}, f32[2,32,128,256]{3,2,1,0:T(8,128)}, f32[2,32,128,256]{3,2,1,0:T(8,128)}) fusion(f32[2,32,128,256]{3,2,1,0:T(8,128)} %copy-done, f32[2,256]{1,0:T(2,128)S(1)} %bitcast.139, f32[2,32,128,256]{3,2,1,0:T(8,128)} %fusion.57, f32[2,256]{1,0:T(2,128)S(1)} %bitcast.140, ...), kind=kOutput, calls=%fused_computation.52 | convolution fusion | flops 2194276352 | bytes 58826752 | tf_op jit(solution)/shard_map/while/body/eval_jaxpr/dot_general | solution.py:100
  455.3 91.2 %collective-permute-done.4 = f32[2,32,16384]{2,1,0:T(8,128)} collective-permute-done((f32[2,32,16384]{2,1,0:T(8,128)}, f32[2,32,16384]{2,1,0:T(8,128)}, u32[]{:S(2)}, u32[]{:S(2)}) %collective-permute-start.4) | collective-permute-done | bytes 4194336 | tf_op jit(solution)/shard_map/ppermute | solution.py:17
  551.3 10.2 %fusion.54 = f32[2,32,128,128]{3,2,1,0:T(8,128)} fusion(f32[2,32,128,256]{3,2,1,0:T(8,128)} %get-tuple-element.58, f32[2,32,128,256]{3,2,1,0:T(8,128)} %get-tuple-element.57), kind=kLoop, calls=%fused_computation.67 | loop fusion | flops 3145728 | bytes 20971520 | tf_op jit(solution)/shard_map/add | solution.py:164
  566.4 32.4 %collective-permute-done.5 = bf16[2,32,16384]{2,1,0:T(8,128)(2,1)} collective-permute-done((bf16[2,32,16384]{2,1,0:T(8,128)(2,1)S(1)}, bf16[2,32,16384]{2,1,0:T(8,128)(2,1)}, u32[]{:S(2)}, u32[]{:S(2)}) %collective-permute-start.5) | collective-permute-done | bytes 2097184 | tf_op jit(solution)/shard_map/ppermute | solution.py:17
  (75 shorter events, 154.8 us)
Async XLA Ops:
  0.0 94.9 %collective-permute-start.1 = (f32[2,32,16384]{2,1,0:T(8,128)}, f32[2,32,16384]{2,1,0:T(8,128)}, u32[]{:S(2)}, u32[]{:S(2)}) collective-permute-start(f32[2,32,16384]{2,1,0:T(8,128)} %param.3), channel_id=1, source_target_pairs={{0,4},{4,8},{8,12},{12,16},{16,20},{20,24},{24,28},{28,32},{32,36}... | collective-permute-start | bytes 12582920 | tf_op jit(solution)/shard_map/ppermute | solution.py:17
  94.9 94.0 %collective-permute-start.3 = (f32[2,32,16384]{2,1,0:T(8,128)}, f32[2,32,16384]{2,1,0:T(8,128)}, u32[]{:S(2)}, u32[]{:S(2)}) collective-permute-start(f32[2,32,16384]{2,1,0:T(8,128)} %collective-permute-done.1), channel_id=1, source_target_pairs={{0,4},{4,8},{8,12},{12,16},{16,20},{20,24},{24,28},{28,32},{32,36}... | collective-permute-start | bytes 12582920 | tf_op jit(solution)/shard_map/ppermute | solution.py:17
  99.2 6.0 copy-start
  135.2 86.7 %all-to-all-start = ((bf16[2,32,128,256]{3,1,0,2:T(8,128)(2,1)}), bf16[2,32,128,256]{3,1,0,2:T(8,128)(2,1)}, u32[]{:S(2)}, u32[]{:S(2)}) async-start(bf16[2,32,128,256]{3,1,0,2:T(8,128)(2,1)} %copy.58), calls=%async_computation | async-start | bytes 8388608 | tf_op jit(solution)/shard_map/while/body/eval_jaxpr/all_to_all | solution.py:93
  221.9 53.4 %all-to-all-start.2 = ((bf16[2,32,128,256]{3,1,0,2:T(8,128)(2,1)}), bf16[2,32,128,256]{3,1,0,2:T(8,128)(2,1)}, u32[]{:S(2)}, u32[]{:S(2)}) async-start(bf16[2,32,128,256]{3,1,0,2:T(8,128)(2,1)} %copy.73), calls=%async_computation.2 | async-start | bytes 8388608 | tf_op jit(solution)/shard_map/while/body/eval_jaxpr/all_to_all | solution.py:93
  246.3 3.5 copy-start.2
  246.3 4.7 copy-start.3
  275.3 53.4 %all-to-all-start.1 = ((bf16[2,128,32,256]{3,2,0,1:T(8,128)(2,1)}), bf16[2,128,32,256]{3,2,0,1:T(8,128)(2,1)}, u32[]{:S(2)}, u32[]{:S(2)}) async-start(bf16[2,128,32,256]{3,2,0,1:T(8,128)(2,1)} %copy.64), calls=%async_computation.1 | async-start | bytes 8388608 | tf_op jit(solution)/shard_map/while/body/eval_jaxpr/all_to_all | solution.py:98
  295.2 3.5 copy-start.1
  295.2 4.7 copy-start.4
  315.0 18.5 %copy-start.6 = (f32[2]{0:T(128)S(1)}, f32[2]{0:T(128)}, u32[]{:S(2)}) copy-start(f32[2]{0:T(128)} %param.4) | copy-start | bytes 28
  315.0 18.6 %copy-start.5 = (s32[2,2,2]{2,1,0:T(2,128)S(1)}, s32[2,2,2]{2,1,0:T(2,128)}, u32[]{:S(2)}) copy-start(s32[2,2,2]{2,1,0:T(2,128)} %param.5) | copy-start | bytes 100
  328.6 56.1 %all-to-all-start.3 = ((bf16[2,128,32,256]{3,2,0,1:T(8,128)(2,1)}), bf16[2,128,32,256]{3,2,0,1:T(8,128)(2,1)}, u32[]{:S(2)}, u32[]{:S(2)}) async-start(bf16[2,128,32,256]{3,2,0,1:T(8,128)(2,1)} %copy.79), calls=%async_computation.3 | async-start | bytes 8388608 | tf_op jit(solution)/shard_map/while/body/eval_jaxpr/all_to_all | solution.py:98
  333.5 21.3 %collective-permute-start = (f32[2]{0:T(128)S(1)}, f32[2]{0:T(128)S(1)}, u32[]{:S(2)}, u32[]{:S(2)}) collective-permute-start(f32[2]{0:T(128)S(1)} %copy-done.6), channel_id=1, source_target_pairs={{0,4},{4,8},{8,12},{12,16},{16,20},{20,24},{24,28},{28,32},{32,36}... | collective-permute-start | bytes 32 | tf_op jit(solution)/shard_map/ppermute | solution.py:17
  354.8 6.1 %collective-permute-start.2 = (f32[2]{0:T(128)S(1)}, f32[2]{0:T(128)S(1)}, u32[]{:S(2)}, u32[]{:S(2)}) collective-permute-start(f32[2]{0:T(128)S(1)} %collective-permute-done), channel_id=1, source_target_pairs={{0,4},{4,8},{8,12},{12,16},{16,20},{20,24},{24,28},{28,32},{32,36}... | collective-permute-start | bytes 32 | tf_op jit(solution)/shard_map/ppermute | solution.py:17
  439.1 107.4 %collective-permute-start.4 = (f32[2,32,16384]{2,1,0:T(8,128)}, f32[2,32,16384]{2,1,0:T(8,128)}, u32[]{:S(2)}, u32[]{:S(2)}) collective-permute-start(f32[2,32,16384]{2,1,0:T(8,128)} %reshape.219), channel_id=1, source_target_pairs={{0,4},{4,8},{8,12},{12,16},{16,20},{20,24},{24,28},{28,32},{32,36}... | collective-permute-start | bytes 12582920 | tf_op jit(solution)/shard_map/ppermute | solution.py:17
  550.3 48.4 %collective-permute-start.5 = (bf16[2,32,16384]{2,1,0:T(8,128)(2,1)S(1)}, bf16[2,32,16384]{2,1,0:T(8,128)(2,1)}, u32[]{:S(2)}, u32[]{:S(2)}) collective-permute-start(bf16[2,32,16384]{2,1,0:T(8,128)(2,1)S(1)} %add_convert_fusion), channel_id=1, source_target_pairs={{0,120},{4,124},{8,0},{12,4},{16,8},{20,12},{24,16},{28,20},{32,24... | collective-permute-start | bytes 6291464 | tf_op jit(solution)/shard_map/ppermute | solution.py:17
where the time goes:
time: 615 us; the launch traced here: 604 us
  waiting for transfers between devices  314 us (51%)
  local copies, waits for them, and re-layouts  161 us (26%)
  matrix products  64.4 us (10%)
  other arithmetic  40.2 us (7%)
  starting transfers between devices  23.5 us (4%)
    ppermute x6, waiting for transfers between devices, shifted(): return lax.ppermute(value, axis, pairs)  292 us
    dot_general x2, matrix products, pair_terms(): jnp.dot(spectrum, inverse_tables[1], preferred_element_type=jnp.float32)  31.4 us
    all_to_all x4, local copies, waits for them, and re-layouts, pair_terms(): lax.all_to_all(spectrum, 'grid', split_axis=2, concat_axis=1, tiled=True)  29.4 us
    all_to_all x4, local copies, waits for them, and re-layouts, pair_terms(): lax.all_to_all(back_lines, 'grid', split_axis=1, concat_axis=2, tiled=True)  22.5 us
    unnamed x24, local copies, waits for them, and re-layouts  16.3 us
    convert_element_type x2, local copies, waits for them, and re-layouts, pair_terms(): spectrum = along_y(forward_tables[0], spectrum).astype(jnp.bfloat16)  15.9 us
    convert_element_type x2, local copies, waits for them, and re-layouts, pair_terms(): back_lines = along_x(inverse_tables[0], screened).astype(jnp.bfloat16)  15.9 us
    slice x8, other arithmetic, rotated(): values[..., half_width:]  15.4 us
  transfers between devices with their start and end apart: 10, of which 8 were waited for; matrix products, arithmetic and copies ran while one was open for 33% of the time, Pallas kernels for 0%

commit v1 on v0

v1 whole, which is shorter than its diff:
```python
import functools
import math

import jax
import jax.numpy as jnp
from jax import lax
from jax.experimental import pallas as pl
from jax.experimental.pallas import tpu as pltpu
from jax.sharding import PartitionSpec as P

GRID = 128
WIDTH = 64.0
NCHUNK = 1
GROUP = 8
AXES = ("band", "grid")
BF = jnp.bfloat16
F32 = jnp.float32


def slot_order(g):
    chip, k = g // 2, g % 2
    return (2 + k, 3 - k, 1 - k, k) if chip == 0 else (k, 1 - k, 3 - k, 2 + k)


def routes(count):
    def pairs(to):
        out = []
        for c in range(count):
            for g in range(4):
                dc, dg = to(g // 2, g % 2)
                out.append((c * 4 + g, ((c + dc) % count) * 4 + dg))
        return out

    first = [
        pairs(lambda chip, k: (-1, 2 + k) if chip == 0 else (0, k)),
        pairs(lambda chip, k: (-1, 3 - k) if chip == 0 else (0, 1 - k)),
        pairs(lambda chip, k: (0, 1 - k) if chip == 0 else (-1, 3 - k)),
        pairs(lambda chip, k: (0, k) if chip == 0 else (-1, 2 + k)),
    ]
    second = [
        pairs(lambda chip, k: (1, 2 * chip + k)),
        pairs(lambda chip, k: (1, 2 * (1 - chip) + k)),
    ]
    core = pairs(lambda chip, k: (0, 2 * chip + 1 - k))
    return first, second, core


def back(pairs):
    return [(d, s) for s, d in pairs]


def send(value, pairs):
    return lax.ppermute(value, AXES, pairs)


def tables():
    index = jnp.arange(GRID, dtype=jnp.int32)
    angle = (index[:, None] * index[None, :] % GRID).astype(F32) * (2.0 * math.pi / GRID)
    cosine, sine = jnp.cos(angle), jnp.sin(angle)
    forward = jnp.concatenate(
        [jnp.concatenate([cosine, -sine], 1), jnp.concatenate([sine, cosine], 1)], 0
    ).astype(BF)
    inverse = jnp.concatenate(
        [jnp.concatenate([cosine, sine], 1), jnp.concatenate([-sine, cosine], 1)], 0
    ).astype(BF)
    return forward, inverse


def screened_kernel():
    index = jnp.arange(GRID, dtype=jnp.int32)
    freq = jnp.where(index >= GRID // 2, index - GRID, index).astype(F32)
    squared = freq[:, None, None] ** 2 + freq[None, :, None] ** 2 + freq[None, None, :] ** 2
    q = squared / WIDTH
    safe = jnp.where(q > 0, q, 1.0)
    ratio = jnp.where(q > 0, -jnp.expm1(-q) / safe, 1.0)
    return ratio * (4.0 / GRID**3)


def dot(left, right):
    return jnp.dot(left, right, preferred_element_type=F32)


def rows_of(parts, lanes, lead=None):
    if lead is None:
        return jnp.concatenate([p[:, lanes] for p in parts], 0)
    return jnp.concatenate([p[lead, :, lanes] for p in parts], 0)


def regroup(value):
    n = GRID
    top = jnp.concatenate([value[:n, :n], value[n:, :n]], 1)
    low = jnp.concatenate([value[:n, n:], value[n:, n:]], 1)
    return jnp.concatenate([top, low], 0)


def forward_body(tx, tz, a0, a1, a2, a3, b0, b1, b2, b3, *w):
    firsts, seconds = (a0, a1, a2, a3), (b0, b1, b2, b3)
    for pair in range(GROUP // 2):
        columns = []
        for half in range(2):
            at = (2 * pair + half) * GRID
            lanes = slice(at, at + GRID)
            own = rows_of(firsts, lanes)
            real = own * rows_of(seconds, lanes, 0)
            imag = own * rows_of(seconds, lanes, 1)
            columns.append(jnp.concatenate([real, imag], 0))
        packed = jnp.concatenate(columns, 1)
        mixed = regroup(dot(tx[...], packed).astype(BF))
        result = dot(mixed, tz[...])
        for half in range(2):
            for i in range(2):
                w[i][2 * pair + half] = result[half * GRID : (half + 1) * GRID, i * GRID : (i + 1) * GRID]


def middle_body(tf, ti, kern, *refs):
    count = 2 * NCHUNK
    parts, outs = (
        [r.reshape(r.shape[0] * 8, GRID) for r in refs[i : i + count]] for i in (0, count)
    )
    rows = GRID // NCHUNK
    for pair in range(4):
        columns = []
        for half in range(2):
            r = 2 * pair + half
            take = [f[pl.ds(r, rows, stride=8), :] for f in parts]
            columns.append(jnp.concatenate(take[0::2] + take[1::2], 0))
        packed = jnp.concatenate(columns, 1).astype(BF)
        spectrum = dot(tf[...], packed)
        factor = jnp.concatenate([kern[2 * pair], kern[2 * pair + 1]], 1)
        factor = jnp.concatenate([factor, factor], 0)
        field = (spectrum * factor).astype(BF)
        result = dot(ti[...], field)
        for half in range(2):
            r = 2 * pair + half
            for i, f in enumerate(outs):
                at = (i % 2) * GRID + (i // 2) * rows
                f[pl.ds(r, rows, stride=8), :] = result[
                    at : at + rows, half * GRID : (half + 1) * GRID
                ]


def inverse_body(weights, tx, tz, u0, u1, a0, a1, a2, a3, b0, b1, b2, b3, *outs):
    firsts, seconds = (a0, a1, a2, a3), (b0, b1, b2, b3)
    own_out, partner_out = outs[:4], outs[4:]
    wo0, wo1, wp0, wp1 = (weights[i] for i in range(4))
    for pair in range(GROUP // 2):
        packed = jnp.concatenate(
            [jnp.concatenate([u[2 * pair], u[2 * pair + 1]], 1) for u in (u0, u1)], 0
        ).astype(BF)
        mixed = regroup(dot(tx[...], packed).astype(BF))
        potential = dot(mixed, tz[...])
        for half in range(2):
            at = (2 * pair + half) * GRID
            lanes = slice(at, at + GRID)
            v0 = potential[half * GRID : (half + 1) * GRID, :GRID]
            v1 = potential[half * GRID : (half + 1) * GRID, GRID:]
            for i in range(4):
                rows = slice(32 * i, 32 * i + 32)
                x0, x1 = v0[rows], v1[rows]
                a = firsts[i][:, lanes].astype(F32)
                p0 = seconds[i][0, :, lanes].astype(F32)
                p1 = seconds[i][1, :, lanes].astype(F32)
                own_out[i][:, lanes] = ((wo0 * x0) * p0 + (wo1 * x1) * p1).astype(BF)
                partner_out[i][0, :, lanes] = ((wp0 * x0) * a).astype(BF)
                partner_out[i][1, :, lanes] = ((wp1 * x1) * a).astype(BF)


def whole(shape):
    return pl.BlockSpec(shape, lambda i: (0,) * len(shape))


def params():
    return pltpu.CompilerParams(
        dimension_semantics=("arbitrary",), vmem_limit_bytes=48 * 1024 * 1024
    )


def forward_call(tx, tz, firsts, seconds):
    lanes = firsts[0].shape[-1]
    ys = lanes // GRID
    step = GROUP * GRID
    return pl.pallas_call(
        forward_body,
        grid=(ys // GROUP,),
        in_specs=[whole((256, 256))] * 2
        + [pl.BlockSpec((32, step), lambda i: (0, i))] * 4
        + [pl.BlockSpec((2, 32, step), lambda i: (0, 0, i))] * 4,
        out_specs=[pl.BlockSpec((GROUP, GRID, GRID), lambda i: (i, 0, 0))] * 2,
        out_shape=[jax.ShapeDtypeStruct((ys, GRID, GRID), F32)] * 2,
        compiler_params=params(),
        name="forward",
    )(tx, tz, *firsts, *seconds)


def middle_call(tf, ti, kern, parts):
    ys = parts[0].shape[0]
    spec = pl.BlockSpec((ys, 8, GRID), lambda i: (0, i, 0))
    return pl.pallas_call(
        middle_body,
        grid=(GRID // 8,),
        in_specs=[whole((256, 256))] * 2
        + [pl.BlockSpec((8, GRID, GRID), lambda i: (i, 0, 0))]
        + [spec] * (2 * NCHUNK),
        out_specs=[spec] * (2 * NCHUNK),
        out_shape=[jax.ShapeDtypeStruct((ys, GRID, GRID), F32)] * (2 * NCHUNK),
        compiler_params=params(),
        name="middle",
    )(tf, ti, kern, *parts)


def inverse_call(weights, tx, tz, u, firsts, seconds):
    lanes = firsts[0].shape[-1]
    step = GROUP * GRID
    one = pl.BlockSpec((32, step), lambda i: (0, i))
    two = pl.BlockSpec((2, 32, step), lambda i: (0, 0, i))
    outs = pl.pallas_call(
        inverse_body,
        grid=(lanes // step,),
        in_specs=[pl.BlockSpec(memory_space=pltpu.SMEM)]
        + [whole((256, 256))] * 2
        + [pl.BlockSpec((GROUP, GRID, GRID), lambda i: (i, 0, 0))] * 2
        + [one] * 4
        + [two] * 4,
        out_specs=[one] * 4 + [two] * 4,
        out_shape=[jax.ShapeDtypeStruct((32, lanes), BF)] * 4
        + [jax.ShapeDtypeStruct((2, 32, lanes), BF)] * 4,
        compiler_params=params(),
        name="inverse",
    )(weights, tx, tz, *u, *firsts, *seconds)
    return outs[:4], outs[4:]


def body(orbitals, occupation, pair_keep):
    count = lax.axis_size("band")
    first_routes, second_routes, core_route = routes(count)
    c, g = lax.axis_index("band"), lax.axis_index("grid")
    chip, k = g // 2, g % 2

    small = jnp.concatenate(
        [occupation[:, None], pair_keep.reshape(2, 4).astype(F32)], 1
    )
    small = lax.all_gather(small, "band")
    lead = small[(c + chip) % count, k]
    partner_occ = small[(c + count - 1) % count, :, 0]
    keep = lax.dynamic_slice(lead, (1 + 2 * chip,), (2,))
    weights = -jnp.concatenate([partner_occ * keep, lead[0] * keep])

    table, table_inv = tables()
    order = jnp.asarray([slot_order(i) for i in range(4)], jnp.int32)[g]
    xs = (order[:, None] * 32 + jnp.arange(32, dtype=jnp.int32)[None]).reshape(-1)
    both = jnp.concatenate([xs, xs + GRID])
    left, left_inv = table.T, table_inv.T
    tx = left[:, both]
    tx_inv = left_inv[both, :]
    kern = screened_kernel()

    lanes = GRID * GRID // NCHUNK
    mine = orbitals.astype(BF)
    firsts, seconds, parts = [], [], []
    for n in range(NCHUNK):
        piece = mine[:, :, n * lanes : (n + 1) * lanes]
        same = lax.dynamic_index_in_dim(piece, k, 0, keepdims=False)
        other = lax.dynamic_index_in_dim(piece, 1 - k, 0, keepdims=False)
        f = [
            send(v, r) for v, r in zip((same, other, other, same), first_routes)
        ]
        s1, s2 = (send(piece, r) for r in second_routes)
        x1, x2 = send(s1, core_route), send(s2, core_route)
        s = [s2, x2, x1, s1]
        firsts.append(f)
        seconds.append(s)
        parts += forward_call(tx, table, f, s)
    fields = middle_call(left, left_inv, kern, parts)
    sames, others = [], []
    for n in range(NCHUNK):
        own, partner = inverse_call(weights, tx_inv, table_inv, fields[2 * n : 2 * n + 2], firsts[n], seconds[n])
        r0, r1, r2, r3 = (send(v, back(r)) for v, r in zip(own, first_routes))
        y0 = send(partner[1], core_route)
        y3 = send(partner[2], core_route)
        sum0 = (partner[0].astype(F32) + y0.astype(F32)).astype(BF)
        sum3 = (partner[3].astype(F32) + y3.astype(F32)).astype(BF)
        p3 = send(sum3, back(second_routes[0])).astype(F32)
        p0 = send(sum0, back(second_routes[1])).astype(F32)
        total = p0 + p3
        same = r0.astype(F32) + r3.astype(F32)
        other = r1.astype(F32) + r2.astype(F32)
        sames.append(jnp.where(k == 0, same, other) + total[0])
        others.append(jnp.where(k == 0, other, same) + total[1])
    return jnp.stack(
        [jnp.concatenate(sames, -1), jnp.concatenate(others, -1)]
    )


def solution(mesh):
    in_specs = (P("band", "grid", None), P("band"), P("band", None, None))
    return jax.shard_map(
        body, mesh=mesh, in_specs=in_specs, out_specs=P("band", "grid", None), check_vma=False
    )
```

time: 615 us -> 409 us (0.67)
  the two profiles are of different devices: /device:TPU:2 before, /device:TPU:8 now
where the time goes in v1:
time: 409 us; the launch traced here: 408 us
  blocking collectives  162 us (40%)
  waiting for transfers between devices  123 us (30%)
  Pallas kernels  61 us (15%)
  starting transfers between devices  25.2 us (6%)
  other arithmetic  22.7 us (6%)
  local copies, waits for them, and re-layouts  13.7 us (3%)
    all_gather x1, blocking collectives, body(): small = lax.all_gather(small, 'band')  162 us
    ppermute x16, waiting for transfers between devices, send(): return lax.ppermute(value, AXES, pairs)  123 us
    ppermute x16, starting transfers between devices, send(): return lax.ppermute(value, AXES, pairs)  25.2 us
    pallas_call x1, Pallas kernels, middle_call(): pl.pallas_call(middle_body, grid=(GRID // 8,), in_specs=[whole((256, 256)...  22.7 us
    pallas_call x1, Pallas kernels, inverse_call(): pl.pallas_call(inverse_body, grid=(lanes // step,), in_specs=[pl.BlockSpe...  20.1 us
    pallas_call x1, Pallas kernels, forward_call(): pl.pallas_call(forward_body, grid=(ys // GROUP,), in_specs=[whole((256, 2...  18.2 us
  transfers between devices with their start and end apart: 16, of which 5 were waited for; matrix products, arithmetic and copies ran while one was open for 7% of the time, Pallas kernels for 0%

profile of v1, /device:TPU:8, one launch (start us, length us, event | category | flops | bytes accessed | tf_op | source)
XLA Modules:
  0.0 407.6 jit_solution(15252860663849378842)
XLA Ops:
  0.0 3.7 convert_element_type.83
  5.5 1.9 collective-permute-start.6
  7.5 3.0 dynamic-slice_bitcast_fusion
  10.9 6.1 %collective-permute-start.2 = (bf16[32,16384]{1,0:T(8,128)(2,1)}, bf16[32,16384]{1,0:T(8,128)(2,1)S(1)}, u32[]{:S(2)}, u32[]{:S(2)}) collective-permute-start(bf16[32,16384]{1,0:T(8,128)(2,1)} %get-tuple-element.33), channel_id=1, source_target_pairs={{0,1},{1,0},{2,127},{3,126},{4,5},{5,4},{6,3},{7,2},{8,9},{9,8},{1... | collective-permute-start | bytes 3145736 | tf_op jit(solution)/shard_map/ppermute | solution.py:53
  20.0 161.9 %all-gather.1 = f32[32,2,5]{2,1,0:T(2,128)S(1)} all-gather(f32[1,2,5]{2,1,0:T(2,128)S(1)} %maximum_bitcast_fusion), channel_id=2, replica_groups=mesh['band'=32,'grid'=4] {'band'}, dimensions={0}, use_global_device_ids=true | all-gather | bytes 1320 | tf_op jit(solution)/shard_map/all_gather | solution.py:242
  184.0 1.8 gather_fusion.1
  188.4 1.8 gather_fusion
  191.1 2.2 collective-permute-start.3
  193.4 8.0 %fusion.1.kern = f32[128,128,128]{2,1,0:T(8,128)} fusion(f32[128]{0:T(128)S(1)} %fusion.20, f32[128,128]{1,0:T(8,128)S(1)} %broadcast_add_fusion), kind=kLoop, calls=%fused_computation.5 | loop fusion | flops 18874368 | bytes 8454656 | tf_op jit(solution)/shard_map/mul | solution.py:76
  201.4 17.2 %collective-permute-done.3.a3 = bf16[32,16384]{1,0:T(8,128)(2,1)S(1)} collective-permute-done((bf16[32,16384]{1,0:T(8,128)(2,1)}, bf16[32,16384]{1,0:T(8,128)(2,1)S(1)}, u32[]{:S(2)}, u32[]{:S(2)}) %collective-permute-start.3) | collective-permute-done | bytes 1048608 | tf_op jit(solution)/shard_map/ppermute | solution.py:53
  218.6 18.2 %forward.1 = (f32[128,128,128]{2,1,0:T(8,128)}, f32[128,128,128]{2,1,0:T(8,128)}) custom-call(bf16[256,256]{1,0:T(8,128)(2,1)S(1)} %bitcast.36, bf16[256,256]{1,0:T(8,128)(2,1)S(1)} %get-tuple-element.35.tz, bf16[32,16384]{1,0:T(8,128)(2,1)S(1)} %collective-permute-done.a0, bf16[32,16384]{1,0:T(8,128)(2,1)S(1)} %collective-permute-done.1.a1, ...), custom_call_target="tpu_custom_call" | custom-call | tf_op jit(solution)/shard_map/forward/pallas_call | solution.py:182
  236.8 22.7 %middle.1 = (f32[128,128,128]{2,1,0:T(8,128)}, f32[128,128,128]{2,1,0:T(8,128)}) custom-call(bf16[256,256]{1,0:T(8,128)(2,1)S(1)} %copy-done.3, bf16[256,256]{1,0:T(8,128)(2,1)S(1)} %copy.16.ti, f32[128,128,128]{2,1,0:T(8,128)} %fusion.1.kern, f32[128,128,128]{2,1,0:T(8,128)} %get-tuple-element.17.refs_0_, f32[128,128,128]{2,1,0:T(8,128)} %get-tuple-element.18.refs_1_), custom_call_target="tpu_custom_call" | custom-call | tf_op jit(solution)/shard_map/middle/pallas_call | solution.py:198
  259.5 20.1 %inverse.1 = (bf16[32,16384]{1,0:T(8,128)(2,1)S(1)}, bf16[32,16384]{1,0:T(8,128)(2,1)S(1)}, bf16[32,16384]{1,0:T(8,128)(2,1)S(1)}, bf16[32,16384]{1,0:T(8,128)(2...) custom-call(f32[4]{0:T(128)S(1)} %maximum_negate_fusion.weights, ...), custom_call_target="tpu_custom_call" | custom-call | tf_op jit(solution)/shard_map/inverse/pallas_call | solution.py:216
  280.3 3.9 collective-permute-done.12
  284.1 3.4 add_convert_fusion.1
  287.5 1.9 add_convert_fusion
  289.4 6.0 %collective-permute-start.15 = (bf16[2,32,16384]{2,1,0:T(8,128)(2,1)}, bf16[2,32,16384]{2,1,0:T(8,128)(2,1)}, u32[]{:S(2)}, u32[]{:S(2)}) collective-permute-start(bf16[2,32,16384]{2,1,0:T(8,128)(2,1)} %add_convert_fusion), channel_id=1, source_target_pairs={{4,0},{5,1},{6,2},{7,3},{8,4},{9,5},{10,6},{11,7},{12,8},{13,9},{1... | collective-permute-start | bytes 6291464 | tf_op jit(solution)/shard_map/ppermute | solution.py:53
  295.4 1.8 collective-permute-start.10
  298.1 39.2 %collective-permute-done.13 = bf16[2,32,16384]{2,1,0:T(8,128)(2,1)} collective-permute-done((bf16[2,32,16384]{2,1,0:T(8,128)(2,1)}, bf16[2,32,16384]{2,1,0:T(8,128)(2,1)}, u32[]{:S(2)}, u32[]{:S(2)}) %collective-permute-start.13) | collective-permute-done | bytes 2097184 | tf_op jit(solution)/shard_map/ppermute | solution.py:53
  337.2 2.3 collective-permute-start.9
  339.6 44.0 %collective-permute-done.15 = bf16[2,32,16384]{2,1,0:T(8,128)(2,1)} collective-permute-done((bf16[2,32,16384]{2,1,0:T(8,128)(2,1)}, bf16[2,32,16384]{2,1,0:T(8,128)(2,1)}, u32[]{:S(2)}, u32[]{:S(2)}) %collective-permute-start.15) | collective-permute-done | bytes 2097184 | tf_op jit(solution)/shard_map/ppermute | solution.py:53
  383.6 2.6 convert_add_fusion
  386.2 18.6 %collective-permute-done.9 = bf16[32,16384]{1,0:T(8,128)(2,1)S(1)} collective-permute-done((bf16[32,16384]{1,0:T(8,128)(2,1)S(1)}, bf16[32,16384]{1,0:T(8,128)(2,1)S(1)}, u32[]{:S(2)}, u32[]{:S(2)}) %collective-permute-start.9) | collective-permute-done | bytes 1048608 | tf_op jit(solution)/shard_map/ppermute | solution.py:53
  405.6 2.0 copy-done.12
  (75 shorter events, 13.0 us)
Async XLA Ops:
  0.0 18.5 %copy-start.10 = (s32[2,2,2]{2,1,0:T(2,128)S(1)}, s32[2,2,2]{2,1,0:T(2,128)}, u32[]{:S(2)}) copy-start(s32[2,2,2]{2,1,0:T(2,128)} %param.6) | copy-start | bytes 100
  0.0 18.6 %copy-start.13 = (f32[2]{0:T(128)S(1)}, f32[2]{0:T(128)}, u32[]{:S(2)}) copy-start(f32[2]{0:T(128)} %param.5) | copy-start | bytes 28
  3.7 178.9 %collective-permute-start.4 = (bf16[2,32,16384]{2,1,0:T(8,128)(2,1)}, bf16[2,32,16384]{2,1,0:T(8,128)(2,1)}, u32[]{:S(2)}, u32[]{:S(2)}) collective-permute-start(bf16[2,32,16384]{2,1,0:T(8,128)(2,1)} %convert_element_type.83), channel_id=1, source_target_pairs={{0,6},{1,7},{2,4},{3,5},{4,10},{5,11},{6,8},{7,9},{8,14},{9,15},{1... | collective-permute-start | bytes 6291464 | tf_op jit(solution)/shard_map/ppermute | solution.py:53
  5.5 177.1 %collective-permute-start.6 = (bf16[2,32,16384]{2,1,0:T(8,128)(2,1)}, bf16[2,32,16384]{2,1,0:T(8,128)(2,1)}, u32[]{:S(2)}, u32[]{:S(2)}) collective-permute-start(bf16[2,32,16384]{2,1,0:T(8,128)(2,1)} %convert_element_type.83), channel_id=1, source_target_pairs={{0,4},{1,5},{2,6},{3,7},{4,8},{5,9},{6,10},{7,11},{8,12},{9,13},{1... | collective-permute-start | bytes 6291464 | tf_op jit(solution)/shard_map/ppermute | solution.py:53
  10.5 190.9 %collective-permute-start.1 = (bf16[32,16384]{1,0:T(8,128)(2,1)}, bf16[32,16384]{1,0:T(8,128)(2,1)S(1)}, u32[]{:S(2)}, u32[]{:S(2)}) collective-permute-start(bf16[32,16384]{1,0:T(8,128)(2,1)} %get-tuple-element.33), channel_id=1, source_target_pairs={{0,127},{1,126},{2,1},{3,0},{4,3},{5,2},{6,5},{7,4},{8,7},{9,6},{1... | collective-permute-start | bytes 3145736 | tf_op jit(solution)/shard_map/ppermute | solution.py:53
  10.9 190.4 %collective-permute-start.2 = (bf16[32,16384]{1,0:T(8,128)(2,1)}, bf16[32,16384]{1,0:T(8,128)(2,1)S(1)}, u32[]{:S(2)}, u32[]{:S(2)}) collective-permute-start(bf16[32,16384]{1,0:T(8,128)(2,1)} %get-tuple-element.33), channel_id=1, source_target_pairs={{0,1},{1,0},{2,127},{3,126},{4,5},{5,4},{6,3},{7,2},{8,9},{9,8},{1... | collective-permute-start | bytes 3145736 | tf_op jit(solution)/shard_map/ppermute | solution.py:53
  17.0 174.1 %collective-permute-start = (bf16[32,16384]{1,0:T(8,128)(2,1)}, bf16[32,16384]{1,0:T(8,128)(2,1)S(1)}, u32[]{:S(2)}, u32[]{:S(2)}) collective-permute-start(bf16[32,16384]{1,0:T(8,128)(2,1)} %get-tuple-element.34), channel_id=1, source_target_pairs={{0,126},{1,127},{2,0},{3,1},{4,2},{5,3},{6,4},{7,5},{8,6},{9,7},{1... | collective-permute-start | bytes 3145736 | tf_op jit(solution)/shard_map/ppermute | solution.py:53
  182.7 35.9 %collective-permute-start.5 = (bf16[2,32,16384]{2,1,0:T(8,128)(2,1)}, bf16[2,32,16384]{2,1,0:T(8,128)(2,1)}, u32[]{:S(2)}, u32[]{:S(2)}) collective-permute-start(bf16[2,32,16384]{2,1,0:T(8,128)(2,1)} %collective-permute-done.4.b0), channel_id=1, source_target_pairs={{0,1},{1,0},{2,3},{3,2},{4,5},{5,4},{6,7},{7,6},{8,9},{9,8},{10,11... | collective-permute-start | bytes 6291464 | tf_op jit(solution)/shard_map/ppermute | solution.py:53
  182.7 35.8 %collective-permute-start.7 = (bf16[2,32,16384]{2,1,0:T(8,128)(2,1)}, bf16[2,32,16384]{2,1,0:T(8,128)(2,1)}, u32[]{:S(2)}, u32[]{:S(2)}) collective-permute-start(bf16[2,32,16384]{2,1,0:T(8,128)(2,1)} %collective-permute-done.6.b3), channel_id=1, source_target_pairs={{0,1},{1,0},{2,3},{3,2},{4,5},{5,4},{6,7},{7,6},{8,9},{9,8},{10,11... | collective-permute-start | bytes 6291464 | tf_op jit(solution)/shard_map/ppermute | solution.py:53
  191.1 27.4 %copy-start.4 = (bf16[256,256]{0,1:T(8,128)(2,1)S(1)}, bf16[256,256]{0,1:T(8,128)(2,1)}, u32[]{:S(2)}) copy-start(bf16[256,256]{0,1:T(8,128)(2,1)} %copy.17) | copy-start | bytes 393220
  191.1 27.4 %collective-permute-start.3 = (bf16[32,16384]{1,0:T(8,128)(2,1)}, bf16[32,16384]{1,0:T(8,128)(2,1)S(1)}, u32[]{:S(2)}, u32[]{:S(2)}) collective-permute-start(bf16[32,16384]{1,0:T(8,128)(2,1)} %get-tuple-element.34), channel_id=1, source_target_pairs={{0,0},{1,1},{2,126},{3,127},{4,4},{5,5},{6,2},{7,3},{8,8},{9,9},{1... | collective-permute-start | bytes 3145736 | tf_op jit(solution)/shard_map/ppermute | solution.py:53
  201.3 35.4 %copy-start = (bf16[32,16384]{1,0:T(8,128)(2,1)}, bf16[32,16384]{1,0:T(8,128)(2,1)S(1)}, u32[]{:S(2)}) copy-start(bf16[32,16384]{1,0:T(8,128)(2,1)S(1)} %collective-permute-done.1.a1) | copy-start | bytes 3145732
  201.4 35.4 %copy-start.1 = (bf16[32,16384]{1,0:T(8,128)(2,1)}, bf16[32,16384]{1,0:T(8,128)(2,1)S(1)}, u32[]{:S(2)}) copy-start(bf16[32,16384]{1,0:T(8,128)(2,1)S(1)} %collective-permute-done.2.a2) | copy-start | bytes 3145732
  218.5 18.2 %copy-start.2 = (bf16[32,16384]{1,0:T(8,128)(2,1)}, bf16[32,16384]{1,0:T(8,128)(2,1)S(1)}, u32[]{:S(2)}) copy-start(bf16[32,16384]{1,0:T(8,128)(2,1)S(1)} %collective-permute-done.3.a3) | copy-start | bytes 3145732
  236.8 22.7 %copy-start.5 = (bf16[256,256]{1,0:T(8,128)(2,1)S(1)}, bf16[256,256]{1,0:T(8,128)(2,1)}, u32[]{:S(2)}) copy-start(bf16[256,256]{1,0:T(8,128)(2,1)} %gather_fusion) | copy-start | bytes 393220
  279.7 4.5 %collective-permute-start.12 = (bf16[2,32,16384]{2,1,0:T(8,128)(2,1)}, bf16[2,32,16384]{2,1,0:T(8,128)(2,1)S(1)}, u32[]{:S(2)}, u32[]{:S(2)}) collective-permute-start(bf16[2,32,16384]{2,1,0:T(8,128)(2,1)} %get-tuple-element.26), channel_id=1, source_target_pairs={{0,1},{1,0},{2,3},{3,2},{4,5},{5,4},{6,7},{7,6},{8,9},{9,8},{10,11... | collective-permute-start | bytes 6291464 | tf_op jit(solution)/shard_map/ppermute | solution.py:53
  279.8 7.8 %collective-permute-start.14 = (bf16[2,32,16384]{2,1,0:T(8,128)(2,1)}, bf16[2,32,16384]{2,1,0:T(8,128)(2,1)S(1)}, u32[]{:S(2)}, u32[]{:S(2)}) collective-permute-start(bf16[2,32,16384]{2,1,0:T(8,128)(2,1)} %get-tuple-element.28), channel_id=1, source_target_pairs={{0,1},{1,0},{2,3},{3,2},{4,5},{5,4},{6,7},{7,6},{8,9},{9,8},{10,11... | collective-permute-start | bytes 6291464 | tf_op jit(solution)/shard_map/ppermute | solution.py:53
  287.5 49.7 %collective-permute-start.13 = (bf16[2,32,16384]{2,1,0:T(8,128)(2,1)}, bf16[2,32,16384]{2,1,0:T(8,128)(2,1)}, u32[]{:S(2)}, u32[]{:S(2)}) collective-permute-start(bf16[2,32,16384]{2,1,0:T(8,128)(2,1)} %add_convert_fusion.1), channel_id=1, source_target_pairs={{6,0},{7,1},{4,2},{5,3},{10,4},{11,5},{8,6},{9,7},{14,8},{15,9},{1... | collective-permute-start | bytes 6291464 | tf_op jit(solution)/shard_map/ppermute | solution.py:53
  289.4 94.2 %collective-permute-start.15 = (bf16[2,32,16384]{2,1,0:T(8,128)(2,1)}, bf16[2,32,16384]{2,1,0:T(8,128)(2,1)}, u32[]{:S(2)}, u32[]{:S(2)}) collective-permute-start(bf16[2,32,16384]{2,1,0:T(8,128)(2,1)} %add_convert_fusion), channel_id=1, source_target_pairs={{4,0},{5,1},{6,2},{7,3},{8,4},{9,5},{10,6},{11,7},{12,8},{13,9},{1... | collective-permute-start | bytes 6291464 | tf_op jit(solution)/shard_map/ppermute | solution.py:53
  295.4 90.8 %collective-permute-start.10 = (bf16[32,16384]{1,0:T(8,128)(2,1)}, bf16[32,16384]{1,0:T(8,128)(2,1)S(1)}, u32[]{:S(2)}, u32[]{:S(2)}) collective-permute-start(bf16[32,16384]{1,0:T(8,128)(2,1)} %copy-done.7), channel_id=1, source_target_pairs={{127,0},{126,1},{1,2},{0,3},{3,4},{2,5},{5,6},{4,7},{7,8},{6,9},{9... | collective-permute-start | bytes 3145736 | tf_op jit(solution)/shard_map/ppermute | solution.py:53
  297.2 89.0 %collective-permute-start.11 = (bf16[32,16384]{1,0:T(8,128)(2,1)}, bf16[32,16384]{1,0:T(8,128)(2,1)S(1)}, u32[]{:S(2)}, u32[]{:S(2)}) collective-permute-start(bf16[32,16384]{1,0:T(8,128)(2,1)} %copy-done.6), channel_id=1, source_target_pairs={{1,0},{0,1},{127,2},{126,3},{5,4},{4,5},{3,6},{2,7},{9,8},{8,9},{7... | collective-permute-start | bytes 3145736 | tf_op jit(solution)/shard_map/ppermute | solution.py:53
  297.2 89.0 %collective-permute-start.8 = (bf16[32,16384]{1,0:T(8,128)(2,1)S(1)}, bf16[32,16384]{1,0:T(8,128)(2,1)S(1)}, u32[]{:S(2)}, u32[]{:S(2)}) collective-permute-start(bf16[32,16384]{1,0:T(8,128)(2,1)S(1)} %get-tuple-element.21), channel_id=1, source_target_pairs={{126,0},{127,1},{0,2},{1,3},{2,4},{3,5},{4,6},{5,7},{6,8},{7,9},{8... | collective-permute-start | bytes 3145736 | tf_op jit(solution)/shard_map/ppermute | solution.py:53
  337.2 67.6 %copy-start.11 = (f32[2,32,16384]{2,1,0:T(8,128)S(1)}, f32[2,32,16384]{2,1,0:T(8,128)}, u32[]{:S(2)}) copy-start(f32[2,32,16384]{2,1,0:T(8,128)} %custom-call.6) | copy-start | bytes 12582916
  337.2 67.6 %collective-permute-start.9 = (bf16[32,16384]{1,0:T(8,128)(2,1)S(1)}, bf16[32,16384]{1,0:T(8,128)(2,1)S(1)}, u32[]{:S(2)}, u32[]{:S(2)}) collective-permute-start(bf16[32,16384]{1,0:T(8,128)(2,1)S(1)} %get-tuple-element.22), channel_id=1, source_target_pairs={{0,0},{1,1},{126,2},{127,3},{4,4},{5,5},{2,6},{3,7},{8,8},{9,9},{6... | collective-permute-start | bytes 3145736 | tf_op jit(solution)/shard_map/ppermute | solution.py:53
  (6 other events, 48.2 us)

commit v2 on v1

--- a/solution.py
+++ b/solution.py
@@ -15,11 +15,6 @@
 AXES = ("band", "grid")
 BF = jnp.bfloat16
 F32 = jnp.float32
-
-
-def slot_order(g):
-    chip, k = g // 2, g % 2
-    return (2 + k, 3 - k, 1 - k, k) if chip == 0 else (k, 1 - k, 3 - k, 2 + k)
 
 
 def routes(count):
@@ -31,18 +26,11 @@
                 out.append((c * 4 + g, ((c + dc) % count) * 4 + dg))
         return out
 
-    first = [
-        pairs(lambda chip, k: (-1, 2 + k) if chip == 0 else (0, k)),
-        pairs(lambda chip, k: (-1, 3 - k) if chip == 0 else (0, 1 - k)),
-        pairs(lambda chip, k: (0, 1 - k) if chip == 0 else (-1, 3 - k)),
-        pairs(lambda chip, k: (0, k) if chip == 0 else (-1, 2 + k)),
-    ]
-    second = [
-        pairs(lambda chip, k: (1, 2 * chip + k)),
-        pairs(lambda chip, k: (1, 2 * (1 - chip) + k)),
-    ]
-    core = pairs(lambda chip, k: (0, 2 * chip + 1 - k))
-    return first, second, core
+    straight = pairs(lambda p, k: (-1, 2 * p) if k == 0 else (2, 2 * p + 1))
+    crossed = pairs(lambda p, k: (2, 2 * p + 1) if k == 0 else (-1, 2 * p))
+    chip = pairs(lambda p, k: (0, 2 * (1 - p) + k))
+    core = pairs(lambda p, k: (0, 2 * p + 1 - k))
+    return straight, crossed, chip, core
 
 
 def back(pairs):
@@ -232,63 +220,62 @@
 
 def body(orbitals, occupation, pair_keep):
     count = lax.axis_size("band")
-    first_routes, second_routes, core_route = routes(count)
-    c, g = lax.axis_index("band"), lax.axis_index("grid")
-    chip, k = g // 2, g % 2
+    straight, crossed, chip_route, core_route = routes(count)
+    g = lax.axis_index("grid")
+    p, k = g // 2, g % 2
 
     small = jnp.concatenate(
         [occupation[:, None], pair_keep.reshape(2, 4).astype(F32)], 1
     )
-    small = lax.all_gather(small, "band")
-    lead = small[(c + chip) % count, k]
-    partner_occ = small[(c + count - 1) % count, :, 0]
-    keep = lax.dynamic_slice(lead, (1 + 2 * chip,), (2,))
-    weights = -jnp.concatenate([partner_occ * keep, lead[0] * keep])
+    lead = lax.dynamic_index_in_dim(send(small, straight), p, 0, keepdims=False)
+    far_keep = lax.dynamic_index_in_dim(small[:, 3:], p, 1, keepdims=False)
+    keep = jnp.where(k == 0, lead[1:3], far_keep)
+    weights = -jnp.concatenate([small[:, 0] * keep, lead[0] * keep])
 
     table, table_inv = tables()
-    order = jnp.asarray([slot_order(i) for i in range(4)], jnp.int32)[g]
-    xs = (order[:, None] * 32 + jnp.arange(32, dtype=jnp.int32)[None]).reshape(-1)
+    xs = ((g ^ jnp.arange(4))[:, None] * 32 + jnp.arange(32)[None]).reshape(-1)
     both = jnp.concatenate([xs, xs + GRID])
     left, left_inv = table.T, table_inv.T
     tx = left[:, both]
     tx_inv = left_inv[both, :]
     kern = screened_kernel()
 
+    def pick(value, band):
+        return lax.dynamic_index_in_dim(value, band, 0, keepdims=False)
+
     lanes = GRID * GRID // NCHUNK
     mine = orbitals.astype(BF)
     firsts, seconds, parts = [], [], []
     for n in range(NCHUNK):
         piece = mine[:, :, n * lanes : (n + 1) * lanes]
-        same = lax.dynamic_index_in_dim(piece, k, 0, keepdims=False)
-        other = lax.dynamic_index_in_dim(piece, 1 - k, 0, keepdims=False)
+        away = send(piece, chip_route)
         f = [
-            send(v, r) for v, r in zip((same, other, other, same), first_routes)
+            send(v, r)
+            for v in (pick(piece, p), pick(away, p))
+            for r in (straight, crossed)
         ]
-        s1, s2 = (send(piece, r) for r in second_routes)
-        x1, x2 = send(s1, core_route), send(s2, core_route)
-        s = [s2, x2, x1, s1]
+        s = [piece, send(piece, core_route), away, send(away, core_route)]
         firsts.append(f)
         seconds.append(s)
         parts += forward_call(tx, table, f, s)
     fields = middle_call(left, left_inv, kern, parts)
-    sames, others = [], []
+    outs = []
     for n in range(NCHUNK):
-        own, partner = inverse_call(weights, tx_inv, table_inv, fields[2 * n : 2 * n + 2], firsts[n], seconds[n])
-        r0, r1, r2, r3 = (send(v, back(r)) for v, r in zip(own, first_routes))
-        y0 = send(partner[1], core_route)
-        y3 = send(partner[2], core_route)
-        sum0 = (partner[0].astype(F32) + y0.astype(F32)).astype(BF)
-        sum3 = (partner[3].astype(F32) + y3.astype(F32)).astype(BF)
-        p3 = send(sum3, back(second_routes[0])).astype(F32)
-        p0 = send(sum0, back(second_routes[1])).astype(F32)
-        total = p0 + p3
-        same = r0.astype(F32) + r3.astype(F32)
-        other = r1.astype(F32) + r2.astype(F32)
-        sames.append(jnp.where(k == 0, same, other) + total[0])
-        others.append(jnp.where(k == 0, other, same) + total[1])
-    return jnp.stack(
-        [jnp.concatenate(sames, -1), jnp.concatenate(others, -1)]
-    )
+        own, partner = inverse_call(
+            weights, tx_inv, table_inv, fields[2 * n : 2 * n + 2], firsts[n], seconds[n]
+        )
+        r0, r1, r2, r3 = (
+            send(v, back(r)).astype(F32) for v, r in zip(own, (straight, crossed) * 2)
+        )
+        sums = [
+            partner[i].astype(F32) + send(partner[i + 1], core_route).astype(F32)
+            for i in (0, 2)
+        ]
+        is_band = (jnp.arange(2) == p)[:, None, None]
+        near = sums[0] + jnp.where(is_band, (r0 + r1)[None], 0.0)
+        far = sums[1] + jnp.where(is_band, (r2 + r3)[None], 0.0)
+        outs.append(near + send(far.astype(BF), chip_route).astype(F32))
+    return jnp.concatenate(outs, -1)
 
 
 def solution(mesh):

time: 409 us -> 321 us (0.78)
  the two profiles are of different devices: /device:TPU:8 before, /device:TPU:105 now
where the time goes in v2:
time: 321 us; the launch traced here: 320 us
  waiting for transfers between devices  190 us (59%)
  Pallas kernels  61.2 us (19%)
  starting transfers between devices  34.7 us (11%)
  other arithmetic  18.1 us (6%)
  local copies, waits for them, and re-layouts  15.4 us (5%)
    ppermute x15, waiting for transfers between devices, send(): return lax.ppermute(value, AXES, pairs)  190 us
    ppermute x15, starting transfers between devices, send(): return lax.ppermute(value, AXES, pairs)  34.7 us
    pallas_call x1, Pallas kernels, middle_call(): pl.pallas_call(middle_body, grid=(GRID // 8,), in_specs=[whole((256, 256)...  22.7 us
    pallas_call x1, Pallas kernels, inverse_call(): pl.pallas_call(inverse_body, grid=(lanes // step,), in_specs=[pl.BlockSpe...  20.1 us
    pallas_call x1, Pallas kernels, forward_call(): pl.pallas_call(forward_body, grid=(ys // GROUP,), in_specs=[whole((256, 2...  18.4 us
    mul x1, other arithmetic, screened_kernel(): return ratio * (4.0 / GRID ** 3)  7.8 us
  transfers between devices with their start and end apart: 15, of which 7 were waited for; matrix products, arithmetic and copies ran while one was open for 8% of the time, Pallas kernels for 0%

profile of v2, /device:TPU:105, one launch (start us, length us, event | category | flops | bytes accessed | tf_op | source)
XLA Modules:
  0.0 320.0 jit_solution(13722931412012773790)
XLA Ops:
  0.0 3.7 %convert_element_type.77.b0 = bf16[2,32,16384]{2,1,0:T(8,128)(2,1)} convert(f32[2,32,16384]{2,1,0:T(8,128)} %param.3) | non-fusion elementwise | flops 1048576 | bytes 6291456 | tf_op jit(solution)/shard_map/convert_element_type | solution.py:247
  3.9 2.4 dynamic-slice_bitcast_fusion.1
  7.5 3.1 collective-permute-start.6
  10.8 1.6 collective-permute-start
  13.2 7.8 %fusion.1.kern = f32[128,128,128]{2,1,0:T(8,128)} fusion(f32[128]{0:T(128)S(1)} %fusion.13, f32[128,128]{1,0:T(8,128)S(1)} %broadcast_add_fusion), kind=kLoop, calls=%fused_computation.5 | loop fusion | flops 18874368 | bytes 8454656 | tf_op jit(solution)/shard_map/mul | solution.py:64
  21.0 61.3 %collective-permute-done.3.b2 = bf16[2,32,16384]{2,1,0:T(8,128)(2,1)} collective-permute-done((bf16[2,32,16384]{2,1,0:T(8,128)(2,1)}, bf16[2,32,16384]{2,1,0:T(8,128)(2,1)}, u32[]{:S(2)}, u32[]{:S(2)}) %collective-permute-start.3) | collective-permute-done | bytes 2097184 | tf_op jit(solution)/shard_map/ppermute | solution.py:41
  82.2 3.6 %collective-permute-start.7 = (bf16[2,32,16384]{2,1,0:T(8,128)(2,1)}, bf16[2,32,16384]{2,1,0:T(8,128)(2,1)}, u32[]{:S(2)}, u32[]{:S(2)}) collective-permute-start(bf16[2,32,16384]{2,1,0:T(8,128)(2,1)} %collective-permute-done.3.b2), channel_id=1, source_target_pairs={{0,1},{1,0},{2,3},{3,2},{4,5},{5,4},{6,7},{7,6},{8,9},{9,8},{10,11... | collective-permute-start | bytes 6291464 | tf_op jit(solution)/shard_map/ppermute | solution.py:41
  85.8 2.3 dynamic-slice_bitcast_fusion
  91.5 1.8 gather_fusion.1
  93.3 1.7 copy.11
  96.1 1.8 gather_fusion
  99.4 35.7 %collective-permute-done.4.a2 = bf16[32,16384]{1,0:T(8,128)(2,1)S(1)} collective-permute-done((bf16[32,16384]{1,0:T(8,128)(2,1)}, bf16[32,16384]{1,0:T(8,128)(2,1)S(1)}, u32[]{:S(2)}, u32[]{:S(2)}) %collective-permute-start.4) | collective-permute-done | bytes 1048608 | tf_op jit(solution)/shard_map/ppermute | solution.py:41
  137.3 18.4 %forward.1 = (f32[128,128,128]{2,1,0:T(8,128)}, f32[128,128,128]{2,1,0:T(8,128)}) custom-call(bf16[256,256]{1,0:T(8,128)(2,1)S(1)} %bitcast.19, bf16[256,256]{1,0:T(8,128)(2,1)S(1)} %get-tuple-element.29.tz, bf16[32,16384]{1,0:T(8,128)(2,1)S(1)} %collective-permute-done.1.a0, bf16[32,16384]{1,0:T(8,128)(2,1)S(1)} %collective-permute-done.2.a1, ...), custom_call_target="tpu_custom_call" | custom-call | tf_op jit(solution)/shard_map/forward/pallas_call | solution.py:170
  155.7 22.7 %middle.1 = (f32[128,128,128]{2,1,0:T(8,128)}, f32[128,128,128]{2,1,0:T(8,128)}) custom-call(bf16[256,256]{1,0:T(8,128)(2,1)S(1)} %copy-done.2, bf16[256,256]{1,0:T(8,128)(2,1)S(1)} %copy.10.ti, f32[128,128,128]{2,1,0:T(8,128)} %fusion.1.kern, f32[128,128,128]{2,1,0:T(8,128)} %get-tuple-element.17.refs_0_, f32[128,128,128]{2,1,0:T(8,128)} %get-tuple-element.18.refs_1_), custom_call_target="tpu_custom_call" | custom-call | tf_op jit(solution)/shard_map/middle/pallas_call | solution.py:186
  178.4 20.1 %inverse.1 = (bf16[32,16384]{1,0:T(8,128)(2,1)S(1)}, bf16[32,16384]{1,0:T(8,128)(2,1)S(1)}, bf16[32,16384]{1,0:T(8,128)(2,1)S(1)}, bf16[32,16384]{1,0:T(8,128)(2...) custom-call(f32[4]{0:T(128)S(1)} %maximum_negate_fusion.weights, ...), custom_call_target="tpu_custom_call" | custom-call | tf_op jit(solution)/shard_map/inverse/pallas_call | solution.py:204
  198.5 9.2 %collective-permute-start.12 = (bf16[32,16384]{1,0:T(8,128)(2,1)S(1)}, bf16[32,16384]{1,0:T(8,128)(2,1)S(1)}, u32[]{:S(2)}, u32[]{:S(2)}) collective-permute-start(bf16[32,16384]{1,0:T(8,128)(2,1)S(1)} %get-tuple-element.27), channel_id=1, source_target_pairs={{124,0},{9,1},{126,2},{11,3},{0,4},{13,5},{2,6},{15,7},{4,8},{17,9... | collective-permute-start | bytes 3145736 | tf_op jit(solution)/shard_map/ppermute | solution.py:41
  207.9 9.1 %collective-permute-start.9 = (bf16[32,16384]{1,0:T(8,128)(2,1)S(1)}, bf16[32,16384]{1,0:T(8,128)(2,1)S(1)}, u32[]{:S(2)}, u32[]{:S(2)}) collective-permute-start(bf16[32,16384]{1,0:T(8,128)(2,1)S(1)} %get-tuple-element.23), channel_id=1, source_target_pairs={{124,0},{9,1},{126,2},{11,3},{0,4},{13,5},{2,6},{15,7},{4,8},{17,9... | collective-permute-start | bytes 3145736 | tf_op jit(solution)/shard_map/ppermute | solution.py:41
  216.9 2.6 collective-permute-done.12
  219.5 2.3 collective-permute-start.8
  221.8 25.2 %collective-permute-done.13 = bf16[32,16384]{1,0:T(8,128)(2,1)S(1)} collective-permute-done((bf16[32,16384]{1,0:T(8,128)(2,1)S(1)}, bf16[32,16384]{1,0:T(8,128)(2,1)S(1)}, u32[]{:S(2)}, u32[]{:S(2)}) %collective-permute-start.13) | collective-permute-done | bytes 1048608 | tf_op jit(solution)/shard_map/ppermute | solution.py:41
  248.1 4.3 %collective-permute-start.14 = (bf16[2,32,16384]{2,1,0:T(8,128)(2,1)S(1)}, bf16[2,32,16384]{2,1,0:T(8,128)(2,1)S(1)}, u32[]{:S(2)}, u32[]{:S(2)}) collective-permute-start(bf16[2,32,16384]{2,1,0:T(8,128)(2,1)S(1)} %add_convert_fusion), channel_id=1, source_target_pairs={{0,2},{1,3},{2,0},{3,1},{4,6},{5,7},{6,4},{7,5},{8,10},{9,11},{10,... | collective-permute-start | bytes 6291464 | tf_op jit(solution)/shard_map/ppermute | solution.py:41
  252.4 24.7 %collective-permute-done.10 = bf16[32,16384]{1,0:T(8,128)(2,1)S(1)} collective-permute-done((bf16[32,16384]{1,0:T(8,128)(2,1)S(1)}, bf16[32,16384]{1,0:T(8,128)(2,1)S(1)}, u32[]{:S(2)}, u32[]{:S(2)}) %collective-permute-start.10) | collective-permute-done | bytes 1048608 | tf_op jit(solution)/shard_map/ppermute | solution.py:41
  277.4 39.6 %collective-permute-done.14 = bf16[2,32,16384]{2,1,0:T(8,128)(2,1)S(1)} collective-permute-done((bf16[2,32,16384]{2,1,0:T(8,128)(2,1)S(1)}, bf16[2,32,16384]{2,1,0:T(8,128)(2,1)S(1)}, u32[]{:S(2)}, u32[]{:S(2)}) %collective-permute-start.14) | collective-permute-done | bytes 2097184 | tf_op jit(solution)/shard_map/ppermute | solution.py:41
  316.9 3.0 convert_add_fusion
  (65 shorter events, 11.9 us)
Async XLA Ops:
  0.0 10.6 %copy-start.7 = (s32[2,2,2]{2,1,0:T(2,128)S(1)}, s32[2,2,2]{2,1,0:T(2,128)}, u32[]{:S(2)}) copy-start(s32[2,2,2]{2,1,0:T(2,128)} %param.5) | copy-start | bytes 100
  0.0 10.7 %copy-start.8 = (f32[2]{0:T(128)S(1)}, f32[2]{0:T(128)}, u32[]{:S(2)}) copy-start(f32[2]{0:T(128)} %param.4) | copy-start | bytes 28
  3.7 78.5 %collective-permute-start.3 = (bf16[2,32,16384]{2,1,0:T(8,128)(2,1)}, bf16[2,32,16384]{2,1,0:T(8,128)(2,1)}, u32[]{:S(2)}, u32[]{:S(2)}) collective-permute-start(bf16[2,32,16384]{2,1,0:T(8,128)(2,1)} %convert_element_type.77.b0), channel_id=1, source_target_pairs={{0,2},{1,3},{2,0},{3,1},{4,6},{5,7},{6,4},{7,5},{8,10},{9,11},{10,... | collective-permute-start | bytes 6291464 | tf_op jit(solution)/shard_map/ppermute | solution.py:41
  6.3 81.8 %collective-permute-start.1 = (bf16[32,16384]{1,0:T(8,128)(2,1)}, bf16[32,16384]{1,0:T(8,128)(2,1)S(1)}, u32[]{:S(2)}, u32[]{:S(2)}) collective-permute-start(bf16[32,16384]{1,0:T(8,128)(2,1)} %dynamic-slice_bitcast_fusion.1), channel_id=1, source_target_pairs={{0,124},{1,9},{2,126},{3,11},{4,0},{5,13},{6,2},{7,15},{8,4},{9,17... | collective-permute-start | bytes 3145736 | tf_op jit(solution)/shard_map/ppermute | solution.py:41
  7.5 91.9 %collective-permute-start.2 = (bf16[32,16384]{1,0:T(8,128)(2,1)}, bf16[32,16384]{1,0:T(8,128)(2,1)S(1)}, u32[]{:S(2)}, u32[]{:S(2)}) collective-permute-start(bf16[32,16384]{1,0:T(8,128)(2,1)} %dynamic-slice_bitcast_fusion.1), channel_id=1, source_target_pairs={{0,9},{1,124},{2,11},{3,126},{4,13},{5,0},{6,15},{7,2},{8,17},{9,4... | collective-permute-start | bytes 3145736 | tf_op jit(solution)/shard_map/ppermute | solution.py:41
  7.5 91.9 %collective-permute-start.6 = (bf16[2,32,16384]{2,1,0:T(8,128)(2,1)}, bf16[2,32,16384]{2,1,0:T(8,128)(2,1)}, u32[]{:S(2)}, u32[]{:S(2)}) collective-permute-start(bf16[2,32,16384]{2,1,0:T(8,128)(2,1)} %convert_element_type.77.b0), channel_id=1, source_target_pairs={{0,1},{1,0},{2,3},{3,2},{4,5},{5,4},{6,7},{7,6},{8,9},{9,8},{10,11... | collective-permute-start | bytes 6291464 | tf_op jit(solution)/shard_map/ppermute | solution.py:41
  10.8 77.3 %collective-permute-start = (f32[2,5]{1,0:T(2,128)S(1)}, f32[2,5]{1,0:T(2,128)S(1)}, u32[]{:S(2)}, u32[]{:S(2)}) collective-permute-start(f32[2,5]{1,0:T(2,128)S(1)} %pad_maximum_fusion.4), channel_id=1, source_target_pairs={{0,124},{1,9},{2,126},{3,11},{4,0},{5,13},{6,2},{7,15},{8,4},{9,17... | collective-permute-start | bytes 128 | tf_op jit(solution)/shard_map/ppermute | solution.py:41
  82.2 54.1 %collective-permute-start.7 = (bf16[2,32,16384]{2,1,0:T(8,128)(2,1)}, bf16[2,32,16384]{2,1,0:T(8,128)(2,1)}, u32[]{:S(2)}, u32[]{:S(2)}) collective-permute-start(bf16[2,32,16384]{2,1,0:T(8,128)(2,1)} %collective-permute-done.3.b2), channel_id=1, source_target_pairs={{0,1},{1,0},{2,3},{3,2},{4,5},{5,4},{6,7},{7,6},{8,9},{9,8},{10,11... | collective-permute-start | bytes 6291464 | tf_op jit(solution)/shard_map/ppermute | solution.py:41
  88.1 46.9 %collective-permute-start.4 = (bf16[32,16384]{1,0:T(8,128)(2,1)}, bf16[32,16384]{1,0:T(8,128)(2,1)S(1)}, u32[]{:S(2)}, u32[]{:S(2)}) collective-permute-start(bf16[32,16384]{1,0:T(8,128)(2,1)} %dynamic-slice_bitcast_fusion), channel_id=1, source_target_pairs={{0,124},{1,9},{2,126},{3,11},{4,0},{5,13},{6,2},{7,15},{8,4},{9,17... | collective-permute-start | bytes 3145736 | tf_op jit(solution)/shard_map/ppermute | solution.py:41
  88.1 48.3 %collective-permute-start.5 = (bf16[32,16384]{1,0:T(8,128)(2,1)}, bf16[32,16384]{1,0:T(8,128)(2,1)}, u32[]{:S(2)}, u32[]{:S(2)}) collective-permute-start(bf16[32,16384]{1,0:T(8,128)(2,1)} %dynamic-slice_bitcast_fusion), channel_id=1, source_target_pairs={{0,9},{1,124},{2,11},{3,126},{4,13},{5,0},{6,15},{7,2},{8,17},{9,4... | collective-permute-start | bytes 3145736 | tf_op jit(solution)/shard_map/ppermute | solution.py:41
  99.4 56.3 %copy-start = (bf16[32,16384]{1,0:T(8,128)(2,1)}, bf16[32,16384]{1,0:T(8,128)(2,1)S(1)}, u32[]{:S(2)}) copy-start(bf16[32,16384]{1,0:T(8,128)(2,1)S(1)} %collective-permute-done.2.a1) | copy-start | bytes 3145732
  135.1 20.6 %copy-start.1 = (bf16[32,16384]{1,0:T(8,128)(2,1)}, bf16[32,16384]{1,0:T(8,128)(2,1)S(1)}, u32[]{:S(2)}) copy-start(bf16[32,16384]{1,0:T(8,128)(2,1)S(1)} %collective-permute-done.4.a2) | copy-start | bytes 3145732
  136.4 0.9 copy-start.3
  137.3 18.4 %copy-start.2 = (bf16[256,256]{1,0:T(8,128)(2,1)S(1)}, bf16[256,256]{1,0:T(8,128)(2,1)}, u32[]{:S(2)}) copy-start(bf16[256,256]{1,0:T(8,128)(2,1)} %copy.12.tf) | copy-start | bytes 393220
  155.7 22.7 %copy-start.4 = (bf16[256,256]{1,0:T(8,128)(2,1)S(1)}, bf16[256,256]{1,0:T(8,128)(2,1)}, u32[]{:S(2)}) copy-start(bf16[256,256]{1,0:T(8,128)(2,1)} %gather_fusion) | copy-start | bytes 393220
  198.5 48.7 %copy-start.6 = (bf16[2,32,16384]{2,1,0:T(8,128)(2,1)S(1)}, bf16[2,32,16384]{2,1,0:T(8,128)(2,1)}, u32[]{:S(2)}) copy-start(bf16[2,32,16384]{2,1,0:T(8,128)(2,1)} %get-tuple-element.25) | copy-start | bytes 6291460
  198.5 21.0 %collective-permute-start.12 = (bf16[32,16384]{1,0:T(8,128)(2,1)S(1)}, bf16[32,16384]{1,0:T(8,128)(2,1)S(1)}, u32[]{:S(2)}, u32[]{:S(2)}) collective-permute-start(bf16[32,16384]{1,0:T(8,128)(2,1)S(1)} %get-tuple-element.27), channel_id=1, source_target_pairs={{124,0},{9,1},{126,2},{11,3},{0,4},{13,5},{2,6},{15,7},{4,8},{17,9... | collective-permute-start | bytes 3145736 | tf_op jit(solution)/shard_map/ppermute | solution.py:41
  207.8 39.2 %collective-permute-start.13 = (bf16[32,16384]{1,0:T(8,128)(2,1)S(1)}, bf16[32,16384]{1,0:T(8,128)(2,1)S(1)}, u32[]{:S(2)}, u32[]{:S(2)}) collective-permute-start(bf16[32,16384]{1,0:T(8,128)(2,1)S(1)} %get-tuple-element.28), channel_id=1, source_target_pairs={{9,0},{124,1},{11,2},{126,3},{13,4},{0,5},{15,6},{2,7},{17,8},{4,9... | collective-permute-start | bytes 3145736 | tf_op jit(solution)/shard_map/ppermute | solution.py:41
  207.8 69.3 %collective-permute-start.10 = (bf16[32,16384]{1,0:T(8,128)(2,1)S(1)}, bf16[32,16384]{1,0:T(8,128)(2,1)S(1)}, u32[]{:S(2)}, u32[]{:S(2)}) collective-permute-start(bf16[32,16384]{1,0:T(8,128)(2,1)S(1)} %get-tuple-element.24), channel_id=1, source_target_pairs={{9,0},{124,1},{11,2},{126,3},{13,4},{0,5},{15,6},{2,7},{17,8},{4,9... | collective-permute-start | bytes 3145736 | tf_op jit(solution)/shard_map/ppermute | solution.py:41
  207.9 69.3 %collective-permute-start.9 = (bf16[32,16384]{1,0:T(8,128)(2,1)S(1)}, bf16[32,16384]{1,0:T(8,128)(2,1)S(1)}, u32[]{:S(2)}, u32[]{:S(2)}) collective-permute-start(bf16[32,16384]{1,0:T(8,128)(2,1)S(1)} %get-tuple-element.23), channel_id=1, source_target_pairs={{124,0},{9,1},{126,2},{11,3},{0,4},{13,5},{2,6},{15,7},{4,8},{17,9... | collective-permute-start | bytes 3145736 | tf_op jit(solution)/shard_map/ppermute | solution.py:41
  216.9 30.3 %collective-permute-start.11 = (bf16[2,32,16384]{2,1,0:T(8,128)(2,1)}, bf16[2,32,16384]{2,1,0:T(8,128)(2,1)S(1)}, u32[]{:S(2)}, u32[]{:S(2)}) collective-permute-start(bf16[2,32,16384]{2,1,0:T(8,128)(2,1)} %get-tuple-element.26), channel_id=1, source_target_pairs={{0,1},{1,0},{2,3},{3,2},{4,5},{5,4},{6,7},{7,6},{8,9},{9,8},{10,11... | collective-permute-start | bytes 6291464 | tf_op jit(solution)/shard_map/ppermute | solution.py:41
  219.5 57.8 %collective-permute-start.8 = (bf16[2,32,16384]{2,1,0:T(8,128)(2,1)}, bf16[2,32,16384]{2,1,0:T(8,128)(2,1)S(1)}, u32[]{:S(2)}, u32[]{:S(2)}) collective-permute-start(bf16[2,32,16384]{2,1,0:T(8,128)(2,1)} %get-tuple-element.22), channel_id=1, source_target_pairs={{0,1},{1,0},{2,3},{3,2},{4,5},{5,4},{6,7},{7,6},{8,9},{9,8},{10,11... | collective-permute-start | bytes 6291464 | tf_op jit(solution)/shard_map/ppermute | solution.py:41
  248.1 68.9 %copy-start.5 = (bf16[2,32,16384]{2,1,0:T(8,128)(2,1)S(1)}, bf16[2,32,16384]{2,1,0:T(8,128)(2,1)}, u32[]{:S(2)}) copy-start(bf16[2,32,16384]{2,1,0:T(8,128)(2,1)} %get-tuple-element.21) | copy-start | bytes 6291460
  248.1 68.8 %collective-permute-start.14 = (bf16[2,32,16384]{2,1,0:T(8,128)(2,1)S(1)}, bf16[2,32,16384]{2,1,0:T(8,128)(2,1)S(1)}, u32[]{:S(2)}, u32[]{:S(2)}) collective-permute-start(bf16[2,32,16384]{2,1,0:T(8,128)(2,1)S(1)} %add_convert_fusion), channel_id=1, source_target_pairs={{0,2},{1,3},{2,0},{3,1},{4,6},{5,7},{6,4},{7,5},{8,10},{9,11},{10,... | collective-permute-start | bytes 6291464 | tf_op jit(solution)/shard_map/ppermute | solution.py:41
  (1 other events, 0.5 us)

commit v3 on v0

v3 whole, which is shorter than its diff:
```python
import functools
import math

import jax
import jax.numpy as jnp
import numpy as np
from jax import lax
from jax.experimental import pallas as pl
from jax.experimental.pallas import tpu as pltpu
from jax.sharding import PartitionSpec as P

GRID = 128
SLAB = 32
BLOCKS = 32
HALF_RING = 16
WIDTH = 64.0
CHUNKS = 8
LANES = GRID * GRID // CHUNKS
PAIRS = LANES // (2 * GRID)
TILES = GRID // 8
BF = jnp.bfloat16
F32 = jnp.float32
MESH = pl.DeviceIdType.MESH


def tables():
    index = np.arange(GRID)
    angle = (index[:, None] * index[None, :] % GRID) * (2.0 * math.pi / GRID)
    cosine, sine = np.cos(angle), np.sin(angle)
    forward = np.block([[cosine, -sine], [sine, cosine]])
    return tuple(np.asarray(t, np.float32).astype(BF) for t in (forward, forward.T))


def dot(left, right):
    return jnp.dot(left, right, preferred_element_type=F32)


def regroup(value):
    n = GRID
    top = jnp.concatenate([value[:n, :n], value[n:, :n]], 1)
    low = jnp.concatenate([value[:n, n:], value[n:, n:]], 1)
    return jnp.concatenate([top, low], 0)


def kernel(
    occ, keep, orbitals, plus, minus, out,
    stage, lead, own, real, imag, factor, near_in, far_in, core_in, chip_in, note_out, note_in,
    load_sem, store_sem, send_a, recv_a, send_b, recv_b, note_sem,
):
    c, g = lax.axis_index("band"), lax.axis_index("grid")
    p, k = lax.div(g, 2), lax.rem(g, 2)
    spot = lax.rem(c, HALF_RING)
    odd = lax.rem(c, 2)

    def block(step):
        return lax.rem(c + BLOCKS + step, BLOCKS)

    def flag(condition):
        return jnp.where(condition, 1, 0)

    cross = {
        1: flag(spot == HALF_RING - 1),
        2: flag(spot >= HALF_RING - 2),
        -1: flag(spot == 0),
        -2: flag(spot <= 1),
    }

    def flip(value, bit):
        return value + bit - 2 * value * bit

    def slot_of(quarter):
        return 2 * flip(quarter // 2, p) + flip(quarter % 2, k)

    def remote(source, target, sends, receives, kind, sort, n, device):
        return pltpu.make_async_remote_copy(
            src_ref=source,
            dst_ref=target,
            send_sem=sends.at[kind, n],
            recv_sem=receives.at[sort, n],
            device_id=device,
            device_id_type=MESH,
        )

    other_core = (c, 2 * p + 1 - k)
    other_chip = (c, 2 * (1 - p) + k)

    def load(n):
        lanes = pl.ds(pl.multiple_of(n * LANES, LANES), LANES)
        return pltpu.make_async_copy(orbitals.at[:, :, lanes], stage.at[n], load_sem.at[n])

    def store(n):
        lanes = pl.ds(pl.multiple_of(n * LANES, LANES), LANES)
        return pltpu.make_async_copy(stage.at[n], out.at[:, :, lanes], store_sem.at[n])

    def each(count, step):
        def run(n, carry):
            step(n)
            return carry

        lax.fori_loop(0, count, run, 0)

    each(CHUNKS, lambda n: load(n).start())

    barrier = pltpu.get_barrier_semaphore()

    def greet(band, grid):
        pl.semaphore_signal(barrier, inc=1, device_id=(band, grid), device_id_type=MESH)

    for away in (1, 2, 3):
        greet(c, lax.rem(g + away, 4))
    for step in (1, 2, -1, -2):
        for core in (0, 1):
            greet(block(step), 2 * p + core)

            @pl.when(cross[step] == 1)
            def _(step=step, core=core):
                greet(block(step), 2 * (1 - p) + core)

    pl.semaphore_wait(barrier, 11 + 2 * (cross[1] + cross[2] + cross[-1] + cross[-2]))

    note_out[0:1, :] = jnp.zeros((1, GRID), F32) + occ[p]
    for j in range(2):
        note_out[1 + j : 2 + j, :] = jnp.zeros((1, GRID), F32) + keep[4 * p + j].astype(F32)
    note = pltpu.make_async_remote_copy(
        src_ref=note_out,
        dst_ref=note_in,
        send_sem=note_sem.at[0],
        recv_sem=note_sem.at[1],
        device_id=(lax.rem(c + BLOCKS - 1 + 3 * k, BLOCKS), g),
        device_id_type=MESH,
    )
    note.start()

    def in_exchange(n):
        mine = own.at[n, 0]
        return (
            remote(mine, own.at[n, 2], send_a, recv_a, 0, 2, n, other_chip),
            remote(mine, own.at[n, 1], send_a, recv_a, 1, 1, n, other_core),
            remote(
                own.at[n, 0, p], lead.at[n, k], send_a, recv_a, 2, 3 + k, n, (block(-1), 2 * p)
            ),
            remote(
                own.at[n, 0, p],
                lead.at[n, 1 - k],
                send_a,
                recv_a,
                3,
                4 - k,
                n,
                (block(2), 2 * p + 1),
            ),
        )

    def in_second(n):
        def source(crossing):
            return own.at[n, 2 - 2 * crossing, flip(p, crossing)]

        near, far = cross[-1], cross[2]
        far_slot = jnp.where(odd == 1, 4, 3 - k)
        far_device = (
            lax.rem(c + 2 - odd, BLOCKS),
            2 * flip(p, far) + jnp.where(odd == 1, k, 1),
        )
        return (
            remote(own.at[n, 2], own.at[n, 3], send_a, recv_a, 4, 0, n, other_core),
            remote(
                source(near),
                lead.at[n, 2 + k],
                send_a,
                recv_a,
                5,
                5 + k,
                n,
                (block(-1), 2 * flip(p, near)),
            ),
            remote(
                source(far), lead.at[n, far_slot], send_a, recv_a, 6, 3 + far_slot, n, far_device
            ),
        )

    def in_relay(n):
        return remote(
            lead.at[n, 4], lead.at[n, 3 - k], send_a, recv_a, 7, 6 - k, n, (block(1), 2 * p + 1)
        )

    def arrived_a(ref, sort, n):
        remote(ref, ref, send_a, recv_a, 0, sort, n, other_core).wait_recv()

    def make_factor(n):
        shape = (GRID, GRID)
        rows = lax.broadcasted_iota(jnp.int32, shape, 0)
        columns = lax.broadcasted_iota(jnp.int32, shape, 1)

        def squared(index):
            freq = jnp.where(index >= GRID // 2, index - GRID, index).astype(F32)
            return freq * freq

        base = squared(rows) + squared(columns)

        def plane(i, carry):
            kx = n * (GRID // CHUNKS) + i
            q = (base + squared(jnp.full(shape, kx, jnp.int32))) * (1.0 / WIDTH)
            safe = jnp.where(q > 0, q, 1.0)
            ratio = jnp.where(q > 0, (1.0 - jnp.exp(-safe)) / safe, 1.0)
            factor[kx] = ratio * (4.0 / GRID**3)
            return carry

        lax.fori_loop(0, GRID // CHUNKS, plane, 0)

    def rows_of(y):
        return pl.ds(pl.multiple_of(y * 8, 8), 8)

    def forward(n):
        for pair in range(PAIRS):
            lanes = slice(pair * 2 * GRID, (pair + 1) * 2 * GRID)
            slots = [slot_of(quarter) for quarter in range(4)]
            first = jnp.concatenate([lead[n, s, :, lanes] for s in slots], 0)
            parts = [
                first * jnp.concatenate([own[n, s, j, :, lanes] for s in slots], 0)
                for j in range(2)
            ]
            mixed = regroup(dot(minus[...], jnp.concatenate(parts, 0)).astype(BF))
            result = dot(mixed, plus[...])
            for half in range(2):
                rows = rows_of(n * 2 * PAIRS + 2 * pair + half)
                for t in range(TILES):
                    at = half * GRID + t * 8
                    real[t, rows, :] = result[at : at + 8, :GRID]
                    imag[t, rows, :] = result[at : at + 8, GRID:]

    def in_step(n, carry):
        @pl.when(n < CHUNKS)
        def _():
            load(n).wait()
            own[n, 0] = stage[n].astype(BF)
            for copy in in_exchange(n):
                copy.start()
            make_factor(n)

        @pl.when((n >= 1) & (n < CHUNKS + 1))
        def _():
            arrived_a(own.at[n - 1, 2], 2, n - 1)
            for copy in in_second(n - 1):
                copy.start()

        @pl.when((n >= 2) & (n < CHUNKS + 2) & (odd == 0))
        def _():
            arrived_a(lead.at[n - 2, 4], 7, n - 2)
            in_relay(n - 2).start()

        @pl.when(n >= 3)
        def _():
            m = n - 3
            arrived_a(own.at[m, 1], 1, m)
            arrived_a(own.at[m, 3], 0, m)
            for s in range(4):
                arrived_a(lead.at[m, s], 3 + s, m)
            forward(m)

        return carry

    lax.fori_loop(0, CHUNKS + 3, in_step, 0)

    def middle(step):
        for t in (2 * step, 2 * step + 1):
            for pair in range(4):
                pick = [pl.ds(2 * pair + half, GRID, stride=8) for half in range(2)]
                packed = jnp.concatenate(
                    [jnp.concatenate([w[t, r, :] for r in pick], 1) for w in (real, imag)], 0
                ).astype(BF)
                scale = jnp.concatenate(
                    [factor[t * 8 + 2 * pair], factor[t * 8 + 2 * pair + 1]], 1
                )
                scale = jnp.concatenate([scale, scale], 0)
                field = (dot(minus[...], packed) * scale).astype(BF)
                result = dot(plus[...], field)
                for half in range(2):
                    at = slice(half * GRID, (half + 1) * GRID)
                    real[t, pick[half], :] = result[:GRID, at]
                    imag[t, pick[half], :] = result[GRID:, at]

    each(TILES // 2, middle)

    def in_sent(n):
        for copy in in_exchange(n) + in_second(n):
            copy.wait_send()

        @pl.when(odd == 0)
        def _():
            in_relay(n).wait_send()

    each(CHUNKS, in_sent)

    note.wait()
    weights = []
    for j in range(2):
        kept = jnp.where(k == 0, note_in[1 + j : 2 + j, :], keep[4 * j + 2 + p].astype(F32))
        for amount in (occ[j], note_in[0:1, :]):
            row = -(amount * kept)
            weights.append(jnp.concatenate([row, row], 1))
    own0, lead0, own1, lead1 = weights

    def inverse(n):
        for pair in range(PAIRS):
            lanes = slice(pair * 2 * GRID, (pair + 1) * 2 * GRID)

            def field(w):
                halves = []
                for half in range(2):
                    rows = rows_of(n * 2 * PAIRS + 2 * pair + half)
                    halves.append(jnp.concatenate([w[t, rows, :] for t in range(TILES)], 0))
                return jnp.concatenate(halves, 1)

            packed = jnp.concatenate([field(real), field(imag)], 0).astype(BF)
            mixed = regroup(dot(plus[...], packed).astype(BF))
            potential = dot(mixed, minus[...])
            v0 = jnp.concatenate([potential[:GRID, :GRID], potential[GRID:, :GRID]], 1)
            v1 = jnp.concatenate([potential[:GRID, GRID:], potential[GRID:, GRID:]], 1)
            for quarter in range(4):
                s = slot_of(quarter)
                rows = slice(quarter * SLAB, (quarter + 1) * SLAB)
                x0, x1 = v0[rows], v1[rows]
                a = lead[n, s, :, lanes].astype(F32)
                b0 = own[n, s, 0, :, lanes].astype(F32)
                b1 = own[n, s, 1, :, lanes].astype(F32)
                lead[n, s, :, lanes] = ((own0 * x0) * b0 + (own1 * x1) * b1).astype(BF)
                own[n, s, 0, :, lanes] = ((lead0 * x0) * a).astype(BF)
                own[n, s, 1, :, lanes] = ((lead1 * x1) * a).astype(BF)

    home = lax.rem(c + BLOCKS + 1 - 3 * k, BLOCKS)
    home_cross = jnp.where(k == 0, cross[1], cross[-2])
    hop = k * (1 - odd)

    def out_first(n):
        far = 2 * flip(p, home_cross)
        target = lax.rem(home + hop, BLOCKS)
        return (
            remote(own.at[n, 1], core_in.at[n, 0], send_b, recv_b, 0, 0, n, other_core),
            remote(own.at[n, 3], core_in.at[n, 1], send_b, recv_b, 1, 1, n, other_core),
            remote(lead.at[n, 0], near_in.at[n, k], send_b, recv_b, 2, 2 + k, n, (home, g)),
            remote(
                lead.at[n, 1],
                near_in.at[n, k],
                send_b,
                recv_b,
                3,
                2 + k,
                n,
                (home, 2 * p + 1 - k),
            ),
            remote(
                lead.at[n, 2],
                far_in.at[n, k + hop],
                send_b,
                recv_b,
                4,
                4 + k + hop,
                n,
                (target, far + k),
            ),
            remote(
                lead.at[n, 3],
                far_in.at[n, k + hop],
                send_b,
                recv_b,
                5,
                4 + k + hop,
                n,
                (target, far + 1 - k),
            ),
        )

    def out_relay(n):
        return remote(
            far_in.at[n, 2], far_in.at[n, 1], send_b, recv_b, 6, 5, n, (block(-1), g)
        )

    def out_chip(n):
        return remote(own.at[n, 2], chip_in.at[n], send_b, recv_b, 7, 7, n, other_chip)

    def arrived_b(ref, sort, n):
        remote(ref, ref, send_b, recv_b, 0, sort, n, other_core).wait_recv()

    straight = [cross[-1].astype(F32), cross[2].astype(F32)]

    def out_step(n, carry):
        @pl.when(n < CHUNKS)
        def _():
            inverse(n)
            for copy in out_first(n):
                copy.start()

        @pl.when((n >= 1) & (n < CHUNKS + 1) & (odd == 1))
        def _():
            arrived_b(far_in.at[n - 1, 2], 6, n - 1)
            out_relay(n - 1).start()

        @pl.when((n >= 2) & (n < CHUNKS + 2))
        def _():
            m = n - 2
            arrived_b(core_in.at[m, 1], 1, m)
            arrived_b(far_in.at[m, 0], 4, m)
            arrived_b(far_in.at[m, 1], 5, m)
            sums = own[m, 2].astype(F32) + core_in[m, 1].astype(F32)
            own[m, 2] = sums.astype(BF)
            extra = (1.0 - straight[0]) * far_in[m, 0].astype(F32) + (
                1.0 - straight[1]
            ) * far_in[m, 1].astype(F32)
            mine = jnp.where(p == 0, sums[0], sums[1])
            own[m, 2, p] = (mine + extra).astype(BF)
            out_chip(m).start()

        @pl.when(n >= 4)
        def _():
            m = n - 4
            arrived_b(core_in.at[m, 0], 0, m)
            arrived_b(near_in.at[m, 0], 2, m)
            arrived_b(near_in.at[m, 1], 3, m)
            arrived_b(chip_in.at[m], 7, m)

            def total(band):
                return (
                    own[m, 0, band].astype(F32)
                    + core_in[m, 0, band].astype(F32)
                    + chip_in[m, band].astype(F32)
                )

            extra = straight[0] * far_in[m, 0].astype(F32) + straight[1] * far_in[m, 1].astype(
                F32
            )
            stage[m, p] = (
                total(p) + near_in[m, 0].astype(F32) + near_in[m, 1].astype(F32)
            )
            stage[m, 1 - p] = total(1 - p) + extra
            store(m).start()

        return carry

    lax.fori_loop(0, CHUNKS + 4, out_step, 0)

    def out_sent(n):
        for copy in out_first(n) + (out_chip(n),):
            copy.wait_send()

        @pl.when(odd == 1)
        def _():
            out_relay(n).wait_send()

        store(n).wait()

    each(CHUNKS, out_sent)


def body(orbitals, occupation, pair_keep):
    plus, minus = tables()
    vmem = pl.BlockSpec(memory_space=pltpu.VMEM)
    smem = pl.BlockSpec(memory_space=pltpu.SMEM)
    anywhere = pl.BlockSpec(memory_space=pl.ANY)
    dma = pltpu.SemaphoreType.DMA
    return pl.pallas_call(
        kernel,
        out_shape=jax.ShapeDtypeStruct(orbitals.shape, F32),
        in_specs=[smem, smem, anywhere, vmem, vmem],
        out_specs=anywhere,
        scratch_shapes=[
            pltpu.VMEM((CHUNKS, 2, SLAB, LANES), F32),
            pltpu.VMEM((CHUNKS, 5, SLAB, LANES), BF),
            pltpu.VMEM((CHUNKS, 4, 2, SLAB, LANES), BF),
            pltpu.VMEM((TILES, 8 * GRID, GRID), F32),
            pltpu.VMEM((TILES, 8 * GRID, GRID), F32),
            pltpu.VMEM((GRID, GRID, GRID), F32),
            pltpu.VMEM((CHUNKS, 2, SLAB, LANES), BF),
            pltpu.VMEM((CHUNKS, 3, SLAB, LANES), BF),
            pltpu.VMEM((CHUNKS, 2, 2, SLAB, LANES), BF),
            pltpu.VMEM((CHUNKS, 2, SLAB, LANES), BF),
            pltpu.VMEM((8, GRID), F32),
            pltpu.VMEM((8, GRID), F32),
            dma((CHUNKS,)),
            dma((CHUNKS,)),
            dma((8, CHUNKS)),
            dma((8, CHUNKS)),
            dma((8, CHUNKS)),
            dma((8, CHUNKS)),
            dma((2,)),
        ],
        compiler_params=pltpu.CompilerParams(
            collective_id=0, has_side_effects=True, vmem_limit_bytes=60 * 1024 * 1024
        ),
        name="exchange",
    )(occupation, pair_keep.reshape(-1), orbitals, jnp.asarray(plus), jnp.asarray(minus))


def solution(mesh):
    in_specs = (P("band", "grid", None), P("band"), P("band", None, None))
    return jax.shard_map(
        body, mesh=mesh, in_specs=in_specs, out_specs=P("band", "grid", None), check_vma=False
    )
```

time: 615 us -> 191 us (0.31)
  the two profiles are of different devices: /device:TPU:2 before, /device:TPU:7 now
where the time goes in v3:
time: 191 us
  Pallas kernels  185 us (97%)
  local copies, waits for them, and re-layouts  5.78 us (3%)
    pallas_call x1, Pallas kernels, body(): pl.pallas_call(kernel, out_shape=jax.ShapeDtypeStruct(orbitals.shape, F32...  185 us
    unnamed x1, local copies, waits for them, and re-layouts  4.5 us

profile of v3, /device:TPU:7, one launch (start us, length us, event | category | flops | bytes accessed | tf_op | source)
XLA Modules:
  0.0 191.0 jit_solution(1662340351134693688)
XLA Ops:
  0.0 1.3 reshape.3.keep
  1.3 185.2 %exchange.1 = f32[2,32,16384]{2,1,0:T(8,128)} custom-call(f32[2]{0:T(128)} %occ.1, s32[8]{0:T(128)} %reshape.3.keep, f32[2,32,16384]{2,1,0:T(8,128)} %orbitals.1, bf16[256,256]{1,0:T(8,128)(2,1)} %constant.4.clone.plus, bf16[256,256]{1,0:T(8,128)(2,1)} %constant.5.clone.minus), custom_call_target="tpu_custom_call" | custom-call | tf_op jit(solution)/shard_map/exchange/pallas_call | solution.py:460
  186.5 4.5 %copy.7 = f32[2,32,16384]{2,1,0:T(8,128)} copy(f32[2,32,16384]{2,1,0:T(8,128)} %exchange.1) | data formatting | bytes 8388608

commit v4 on v3

--- a/solution.py
+++ b/solution.py
@@ -14,7 +14,7 @@
 BLOCKS = 32
 HALF_RING = 16
 WIDTH = 64.0
-CHUNKS = 8
+CHUNKS = 16
 LANES = GRID * GRID // CHUNKS
 PAIRS = LANES // (2 * GRID)
 TILES = GRID // 8
@@ -44,7 +44,7 @@
 
 def kernel(
     occ, keep, orbitals, plus, minus, out,
-    stage, lead, own, real, imag, factor, near_in, far_in, core_in, chip_in, note_out, note_in,
+    stage, lead, own, real, imag, factor, sums_in, core_in, chip_in, note_out, note_in,
     load_sem, store_sem, send_a, recv_a, send_b, recv_b, note_sem,
 ):
     c, g = lax.axis_index("band"), lax.axis_index("grid")
@@ -75,7 +75,7 @@
         return pltpu.make_async_remote_copy(
             src_ref=source,
             dst_ref=target,
-            send_sem=sends.at[kind, n],
+            send_sem=sends.at[kind],
             recv_sem=receives.at[sort, n],
             device_id=device,
             device_id_type=MESH,
@@ -86,11 +86,11 @@
 
     def load(n):
         lanes = pl.ds(pl.multiple_of(n * LANES, LANES), LANES)
-        return pltpu.make_async_copy(orbitals.at[:, :, lanes], stage.at[n], load_sem.at[n])
+        return pltpu.make_async_copy(orbitals.at[:, :, lanes], stage.at[n], load_sem.at[0])
 
     def store(n):
         lanes = pl.ds(pl.multiple_of(n * LANES, LANES), LANES)
-        return pltpu.make_async_copy(stage.at[n], out.at[:, :, lanes], store_sem.at[n])
+        return pltpu.make_async_copy(stage.at[n], out.at[:, :, lanes], store_sem.at[0])
 
     def each(count, step):
         def run(n, carry):
@@ -120,7 +120,7 @@
 
     note_out[0:1, :] = jnp.zeros((1, GRID), F32) + occ[p]
     for j in range(2):
-        note_out[1 + j : 2 + j, :] = jnp.zeros((1, GRID), F32) + keep[4 * p + j].astype(F32)
+        note_out[1 + j : 2 + j, :] = jnp.zeros((1, GRID), F32) + keep[p, 0, j].astype(F32)
     note = pltpu.make_async_remote_copy(
         src_ref=note_out,
         dst_ref=note_in,
@@ -131,57 +131,81 @@
     )
     note.start()
 
-    def in_exchange(n):
+    def in_first(n):
+        near, far = cross[-1], cross[2]
         mine = own.at[n, 0]
         return (
-            remote(mine, own.at[n, 2], send_a, recv_a, 0, 2, n, other_chip),
+            remote(mine, own.at[n, 2], send_a, recv_a, 0, 0, n, other_chip),
             remote(mine, own.at[n, 1], send_a, recv_a, 1, 1, n, other_core),
             remote(
-                own.at[n, 0, p], lead.at[n, k], send_a, recv_a, 2, 3 + k, n, (block(-1), 2 * p)
-            ),
-            remote(
-                own.at[n, 0, p],
-                lead.at[n, 1 - k],
+                own.at[n, 0, flip(p, near)],
+                lead.at[n, k + 2 * near],
                 send_a,
                 recv_a,
-                3,
-                4 - k,
-                n,
-                (block(2), 2 * p + 1),
-            ),
-        )
-
-    def in_second(n):
-        def source(crossing):
-            return own.at[n, 2 - 2 * crossing, flip(p, crossing)]
-
-        near, far = cross[-1], cross[2]
-        far_slot = jnp.where(odd == 1, 4, 3 - k)
-        far_device = (
-            lax.rem(c + 2 - odd, BLOCKS),
-            2 * flip(p, far) + jnp.where(odd == 1, k, 1),
-        )
-        return (
-            remote(own.at[n, 2], own.at[n, 3], send_a, recv_a, 4, 0, n, other_core),
-            remote(
-                source(near),
-                lead.at[n, 2 + k],
-                send_a,
-                recv_a,
-                5,
-                5 + k,
+                2,
+                1,
                 n,
                 (block(-1), 2 * flip(p, near)),
             ),
             remote(
-                source(far), lead.at[n, far_slot], send_a, recv_a, 6, 3 + far_slot, n, far_device
+                own.at[n, 0, flip(p, far)],
+                lead.at[n, 1 - k + 2 * far],
+                send_a,
+                recv_a,
+                3,
+                1,
+                n,
+                (block(2), 2 * flip(p, far) + 1),
+            ),
+        )
+
+    def in_second(n):
+        near, far = cross[-1], cross[2]
+        return (
+            remote(own.at[n, 2], own.at[n, 3], send_a, recv_a, 4, 1, n, other_core),
+            remote(
+                own.at[n, 2, flip(p, near)],
+                lead.at[n, k + 2 - 2 * near],
+                send_a,
+                recv_a,
+                5,
+                1,
+                n,
+                (block(-1), 2 * flip(p, near)),
+            ),
+            remote(
+                own.at[n, 2, flip(p, far)],
+                lead.at[n, jnp.where(odd == 1, 4, 3 - k - 2 * far)],
+                send_a,
+                recv_a,
+                6,
+                1 + odd,
+                n,
+                (lax.rem(c + 2 - odd, BLOCKS), 2 * flip(p, far) + jnp.where(odd == 1, k, 1)),
             ),
         )
 
     def in_relay(n):
         return remote(
-            lead.at[n, 4], lead.at[n, 3 - k], send_a, recv_a, 7, 6 - k, n, (block(1), 2 * p + 1)
-        )
+            lead.at[n, 4],
+            lead.at[n, 3 - k - 2 * cross[-1]],
+            send_a,
+            recv_a,
+            7,
+            1,
+            n,
+            (block(1), 2 * p + 1),
+        )
+
+    def sent(ref, sends, kind):
+        pltpu.make_async_remote_copy(
+            src_ref=ref,
+            dst_ref=ref,
+            send_sem=sends.at[kind],
+            recv_sem=note_sem.at[1],
+            device_id=other_core,
+            device_id_type=MESH,
+        ).wait_send()
 
     def arrived_a(ref, sort, n):
         remote(ref, ref, send_a, recv_a, 0, sort, n, other_core).wait_recv()
@@ -228,41 +252,38 @@
                     real[t, rows, :] = result[at : at + 8, :GRID]
                     imag[t, rows, :] = result[at : at + 8, GRID:]
 
+    pltpu.make_async_copy(stage, stage, load_sem.at[0]).wait()
+
     def in_step(n, carry):
         @pl.when(n < CHUNKS)
         def _():
-            load(n).wait()
             own[n, 0] = stage[n].astype(BF)
-            for copy in in_exchange(n):
+            for copy in in_first(n):
                 copy.start()
             make_factor(n)
 
         @pl.when((n >= 1) & (n < CHUNKS + 1))
         def _():
-            arrived_a(own.at[n - 1, 2], 2, n - 1)
+            arrived_a(own.at[n - 1, 2], 0, n - 1)
             for copy in in_second(n - 1):
                 copy.start()
 
         @pl.when((n >= 2) & (n < CHUNKS + 2) & (odd == 0))
         def _():
-            arrived_a(lead.at[n - 2, 4], 7, n - 2)
+            arrived_a(lead.at[n - 2, 4], 2, n - 2)
             in_relay(n - 2).start()
 
         @pl.when(n >= 3)
         def _():
-            m = n - 3
-            arrived_a(own.at[m, 1], 1, m)
-            arrived_a(own.at[m, 3], 0, m)
-            for s in range(4):
-                arrived_a(lead.at[m, s], 3 + s, m)
-            forward(m)
+            arrived_a(own.at[n - 3], 1, n - 3)
+            forward(n - 3)
 
         return carry
 
     lax.fori_loop(0, CHUNKS + 3, in_step, 0)
 
     def middle(step):
-        for t in (2 * step, 2 * step + 1):
+        for t in (4 * step + i for i in range(4)):
             for pair in range(4):
                 pick = [pl.ds(2 * pair + half, GRID, stride=8) for half in range(2)]
                 packed = jnp.concatenate(
@@ -279,22 +300,21 @@
                     real[t, pick[half], :] = result[:GRID, at]
                     imag[t, pick[half], :] = result[GRID:, at]
 
-    each(TILES // 2, middle)
-
-    def in_sent(n):
-        for copy in in_exchange(n) + in_second(n):
-            copy.wait_send()
-
-        @pl.when(odd == 0)
-        def _():
-            in_relay(n).wait_send()
-
-    each(CHUNKS, in_sent)
+    each(TILES // 4, middle)
+
+    for kind, ref in enumerate(
+        (own.at[:, 0],) * 2 + (own.at[:, 0, 0],) * 2 + (own.at[:, 2],) + (own.at[:, 2, 0],) * 2
+    ):
+        sent(ref, send_a, kind)
+
+    @pl.when(odd == 0)
+    def _():
+        sent(lead.at[:, 4], send_a, 7)
 
     note.wait()
     weights = []
     for j in range(2):
-        kept = jnp.where(k == 0, note_in[1 + j : 2 + j, :], keep[4 * j + 2 + p].astype(F32))
+        kept = jnp.where(k == 0, note_in[1 + j : 2 + j, :], keep[j, 1, p].astype(F32))
         for amount in (occ[j], note_in[0:1, :]):
             row = -(amount * kept)
             weights.append(jnp.concatenate([row, row], 1))
@@ -332,56 +352,53 @@
     hop = k * (1 - odd)
 
     def out_first(n):
-        far = 2 * flip(p, home_cross)
-        target = lax.rem(home + hop, BLOCKS)
+        chip = 2 * flip(p, home_cross)
+
+        def lead_out(slot, core):
+            away = slot // 2
+            hands_on = flip(away, home_cross)
+            relayed = away * hop
+            kind = k + 2 * hands_on + relayed * (4 - k - 2 * hands_on)
+            device = (lax.rem(home + relayed, BLOCKS), chip + core)
+            sort = (1 - hands_on) * (1 - relayed) + 2 * relayed
+            return remote(
+                lead.at[n, slot], sums_in.at[n, kind], send_b, recv_b, 2 + slot, sort, n, device
+            )
+
         return (
-            remote(own.at[n, 1], core_in.at[n, 0], send_b, recv_b, 0, 0, n, other_core),
-            remote(own.at[n, 3], core_in.at[n, 1], send_b, recv_b, 1, 1, n, other_core),
-            remote(lead.at[n, 0], near_in.at[n, k], send_b, recv_b, 2, 2 + k, n, (home, g)),
-            remote(
-                lead.at[n, 1],
-                near_in.at[n, k],
-                send_b,
-                recv_b,
-                3,
-                2 + k,
-                n,
-                (home, 2 * p + 1 - k),
-            ),
-            remote(
-                lead.at[n, 2],
-                far_in.at[n, k + hop],
-                send_b,
-                recv_b,
-                4,
-                4 + k + hop,
-                n,
-                (target, far + k),
-            ),
-            remote(
-                lead.at[n, 3],
-                far_in.at[n, k + hop],
-                send_b,
-                recv_b,
-                5,
-                4 + k + hop,
-                n,
-                (target, far + 1 - k),
-            ),
+            remote(own.at[n, 1], core_in.at[n, 0], send_b, recv_b, 0, 1, n, other_core),
+            remote(own.at[n, 3], core_in.at[n, 1], send_b, recv_b, 1, 0, n, other_core),
+            lead_out(0, k),
+            lead_out(1, 1 - k),
+            lead_out(2, k),
+            lead_out(3, 1 - k),
         )
 
     def out_relay(n):
         return remote(
-            far_in.at[n, 2], far_in.at[n, 1], send_b, recv_b, 6, 5, n, (block(-1), g)
+            sums_in.at[n, 4],
+            sums_in.at[n, 3 - 2 * cross[1]],
+            send_b,
+            recv_b,
+            6,
+            cross[1],
+            n,
+            (block(-1), g),
         )
 
     def out_chip(n):
-        return remote(own.at[n, 2], chip_in.at[n], send_b, recv_b, 7, 7, n, other_chip)
+        return remote(own.at[n, 2], chip_in.at[n], send_b, recv_b, 7, 3, n, other_chip)
 
     def arrived_b(ref, sort, n):
         remote(ref, ref, send_b, recv_b, 0, sort, n, other_core).wait_recv()
 
-    straight = [cross[-1].astype(F32), cross[2].astype(F32)]
+    bands = [flip(p, cross[-1]), flip(p, cross[2])]
+    masks = [[flag(b == band).astype(F32) for b in bands] for band in range(2)]
+
+    def lead_sums(m, first, band):
+        return masks[band][0] * sums_in[m, first].astype(F32) + masks[band][1] * sums_in[
+            m, first + 1
+        ].astype(F32)
 
     def out_step(n, carry):
         @pl.when(n < CHUNKS)
@@ -392,63 +409,43 @@
 
         @pl.when((n >= 1) & (n < CHUNKS + 1) & (odd == 1))
         def _():
-            arrived_b(far_in.at[n - 1, 2], 6, n - 1)
+            arrived_b(sums_in.at[n - 1, 4], 2, n - 1)
             out_relay(n - 1).start()
 
         @pl.when((n >= 2) & (n < CHUNKS + 2))
         def _():
             m = n - 2
-            arrived_b(core_in.at[m, 1], 1, m)
-            arrived_b(far_in.at[m, 0], 4, m)
-            arrived_b(far_in.at[m, 1], 5, m)
-            sums = own[m, 2].astype(F32) + core_in[m, 1].astype(F32)
-            own[m, 2] = sums.astype(BF)
-            extra = (1.0 - straight[0]) * far_in[m, 0].astype(F32) + (
-                1.0 - straight[1]
-            ) * far_in[m, 1].astype(F32)
-            mine = jnp.where(p == 0, sums[0], sums[1])
-            own[m, 2, p] = (mine + extra).astype(BF)
+            arrived_b(core_in.at[m], 0, m)
+            for band in range(2):
+                total = own[m, 2, band].astype(F32) + core_in[m, 1, band].astype(F32)
+                own[m, 2, band] = (total + lead_sums(m, 2, band)).astype(BF)
             out_chip(m).start()
 
         @pl.when(n >= 4)
         def _():
             m = n - 4
-            arrived_b(core_in.at[m, 0], 0, m)
-            arrived_b(near_in.at[m, 0], 2, m)
-            arrived_b(near_in.at[m, 1], 3, m)
-            arrived_b(chip_in.at[m], 7, m)
-
-            def total(band):
-                return (
-                    own[m, 0, band].astype(F32)
-                    + core_in[m, 0, band].astype(F32)
-                    + chip_in[m, band].astype(F32)
+            arrived_b(core_in.at[m], 1, m)
+            arrived_b(chip_in.at[m], 3, m)
+            for band in range(2):
+                total = own[m, 0, band].astype(F32) + core_in[m, 0, band].astype(F32)
+                stage[m, band] = (
+                    total + chip_in[m, band].astype(F32) + lead_sums(m, 0, band)
                 )
-
-            extra = straight[0] * far_in[m, 0].astype(F32) + straight[1] * far_in[m, 1].astype(
-                F32
-            )
-            stage[m, p] = (
-                total(p) + near_in[m, 0].astype(F32) + near_in[m, 1].astype(F32)
-            )
-            stage[m, 1 - p] = total(1 - p) + extra
             store(m).start()
 
         return carry
 
     lax.fori_loop(0, CHUNKS + 4, out_step, 0)
 
-    def out_sent(n):
-        for copy in out_first(n) + (out_chip(n),):
-            copy.wait_send()
-
-        @pl.when(odd == 1)
-        def _():
-            out_relay(n).wait_send()
-
-        store(n).wait()
-
-    each(CHUNKS, out_sent)
+    for kind, ref in enumerate((own.at[:, 0],) * 2 + (lead.at[:, 0],) * 4):
+        sent(ref, send_b, kind)
+
+    @pl.when(odd == 1)
+    def _():
+        sent(sums_in.at[:, 4], send_b, 6)
+
+    sent(own.at[:, 2], send_b, 7)
+    pltpu.make_async_copy(stage, stage, store_sem.at[0]).wait()
 
 
 def body(orbitals, occupation, pair_keep):
@@ -469,25 +466,24 @@
             pltpu.VMEM((TILES, 8 * GRID, GRID), F32),
             pltpu.VMEM((TILES, 8 * GRID, GRID), F32),
             pltpu.VMEM((GRID, GRID, GRID), F32),
-            pltpu.VMEM((CHUNKS, 2, SLAB, LANES), BF),
-            pltpu.VMEM((CHUNKS, 3, SLAB, LANES), BF),
+            pltpu.VMEM((CHUNKS, 5, SLAB, LANES), BF),
             pltpu.VMEM((CHUNKS, 2, 2, SLAB, LANES), BF),
             pltpu.VMEM((CHUNKS, 2, SLAB, LANES), BF),
             pltpu.VMEM((8, GRID), F32),
             pltpu.VMEM((8, GRID), F32),
-            dma((CHUNKS,)),
-            dma((CHUNKS,)),
-            dma((8, CHUNKS)),
-            dma((8, CHUNKS)),
-            dma((8, CHUNKS)),
-            dma((8, CHUNKS)),
+            dma((1,)),
+            dma((1,)),
+            dma((8,)),
+            dma((3, CHUNKS)),
+            dma((8,)),
+            dma((4, CHUNKS)),
             dma((2,)),
         ],
         compiler_params=pltpu.CompilerParams(
             collective_id=0, has_side_effects=True, vmem_limit_bytes=60 * 1024 * 1024
         ),
         name="exchange",
-    )(occupation, pair_keep.reshape(-1), orbitals, jnp.asarray(plus), jnp.asarray(minus))
+    )(occupation, pair_keep, orbitals, jnp.asarray(plus), jnp.asarray(minus))
 
 
 def solution(mesh):

time: 191 us -> 178 us (0.932)
  the two profiles are of different devices: /device:TPU:7 before, /device:TPU:8 now
where the time goes in v4:
time: 178 us; the launch traced here: 176 us
  Pallas kernels  172 us (97%)
  local copies, waits for them, and re-layouts  4.5 us (3%)
    pallas_call x1, Pallas kernels, body(): pl.pallas_call(kernel, out_shape=jax.ShapeDtypeStruct(orbitals.shape, F32...  172 us
    unnamed x1, local copies, waits for them, and re-layouts  4.5 us

profile of v4, /device:TPU:8, one launch (start us, length us, event | category | flops | bytes accessed | tf_op | source)
XLA Modules:
  0.0 176.3 jit_solution(13728153616794624780)
XLA Ops:
  0.0 171.8 %exchange.1 = f32[2,32,16384]{2,1,0:T(8,128)} custom-call(f32[2]{0:T(128)} %occ.1, s32[2,2,2]{2,1,0:T(2,128)} %keep.1, f32[2,32,16384]{2,1,0:T(8,128)} %orbitals.1, bf16[256,256]{1,0:T(8,128)(2,1)} %constant.4.clone.plus, bf16[256,256]{1,0:T(8,128)(2,1)} %constant.5.clone.minus), custom_call_target="tpu_custom_call" | custom-call | tf_op jit(solution)/shard_map/exchange/pallas_call | solution.py:457
  171.8 4.5 %copy.7 = f32[2,32,16384]{2,1,0:T(8,128)} copy(f32[2,32,16384]{2,1,0:T(8,128)} %exchange.1) | data formatting | bytes 8388608

commit v5 on v4

--- a/solution.py
+++ b/solution.py
@@ -18,6 +18,9 @@
 LANES = GRID * GRID // CHUNKS
 PAIRS = LANES // (2 * GRID)
 TILES = GRID // 8
+IN_LAGS = (2, 4, 8)
+OUT_LAGS = (2, 2, 3, 5)
+THIRDS = sum(n % 3 == 2 for n in range(CHUNKS))
 BF = jnp.bfloat16
 F32 = jnp.float32
 MESH = pl.DeviceIdType.MESH
@@ -50,7 +53,7 @@
     c, g = lax.axis_index("band"), lax.axis_index("grid")
     p, k = lax.div(g, 2), lax.rem(g, 2)
     spot = lax.rem(c, HALF_RING)
-    odd = lax.rem(c, 2)
+    z = lax.rem(c, 4)
 
     def block(step):
         return lax.rem(c + BLOCKS + step, BLOCKS)
@@ -59,10 +62,8 @@
         return jnp.where(condition, 1, 0)
 
     cross = {
-        1: flag(spot == HALF_RING - 1),
-        2: flag(spot >= HALF_RING - 2),
-        -1: flag(spot == 0),
-        -2: flag(spot <= 1),
+        step: flag(spot >= HALF_RING - step) if step > 0 else flag(spot < -step)
+        for step in (1, 2, 3, -1, -2, -3)
     }
 
     def flip(value, bit):
@@ -101,6 +102,13 @@
 
     each(CHUNKS, lambda n: load(n).start())
 
+    def clear(n):
+        @pl.when((k == 0) | (lax.rem(n, 3) == 2))
+        def _():
+            sums_in[n, 2] = jnp.zeros((SLAB, LANES), BF)
+
+    each(CHUNKS, clear)
+
     barrier = pltpu.get_barrier_semaphore()
 
     def greet(band, grid):
@@ -108,7 +116,7 @@
 
     for away in (1, 2, 3):
         greet(c, lax.rem(g + away, 4))
-    for step in (1, 2, -1, -2):
+    for step in cross:
         for core in (0, 1):
             greet(block(step), 2 * p + core)
 
@@ -116,86 +124,95 @@
             def _(step=step, core=core):
                 greet(block(step), 2 * (1 - p) + core)
 
-    pl.semaphore_wait(barrier, 11 + 2 * (cross[1] + cross[2] + cross[-1] + cross[-2]))
-
-    note_out[0:1, :] = jnp.zeros((1, GRID), F32) + occ[p]
-    for j in range(2):
-        note_out[1 + j : 2 + j, :] = jnp.zeros((1, GRID), F32) + keep[p, 0, j].astype(F32)
+    pl.semaphore_wait(barrier, 15 + 2 * sum(cross.values()))
+
+    note_out[...] = jnp.zeros((8, GRID), F32) + occ[p]
     note = pltpu.make_async_remote_copy(
         src_ref=note_out,
         dst_ref=note_in,
         send_sem=note_sem.at[0],
         recv_sem=note_sem.at[1],
-        device_id=(lax.rem(c + BLOCKS - 1 + 3 * k, BLOCKS), g),
+        device_id=(lax.rem(c + 1 + k, BLOCKS), g),
         device_id_type=MESH,
     )
     note.start()
 
-    def in_first(n):
-        near, far = cross[-1], cross[2]
+    def third(n):
+        return lax.rem(n, 3) == 2
+
+    def in_bands(n):
         mine = own.at[n, 0]
         return (
             remote(mine, own.at[n, 2], send_a, recv_a, 0, 0, n, other_chip),
             remote(mine, own.at[n, 1], send_a, recv_a, 1, 1, n, other_core),
-            remote(
-                own.at[n, 0, flip(p, near)],
-                lead.at[n, k + 2 * near],
-                send_a,
-                recv_a,
-                2,
-                1,
-                n,
-                (block(-1), 2 * flip(p, near)),
-            ),
-            remote(
-                own.at[n, 0, flip(p, far)],
-                lead.at[n, 1 - k + 2 * far],
-                send_a,
-                recv_a,
-                3,
-                1,
-                n,
-                (block(2), 2 * flip(p, far) + 1),
-            ),
-        )
-
-    def in_second(n):
-        near, far = cross[-1], cross[2]
-        return (
-            remote(own.at[n, 2], own.at[n, 3], send_a, recv_a, 4, 1, n, other_core),
-            remote(
-                own.at[n, 2, flip(p, near)],
-                lead.at[n, k + 2 - 2 * near],
-                send_a,
-                recv_a,
-                5,
-                1,
-                n,
-                (block(-1), 2 * flip(p, near)),
-            ),
-            remote(
-                own.at[n, 2, flip(p, far)],
-                lead.at[n, jnp.where(odd == 1, 4, 3 - k - 2 * far)],
-                send_a,
-                recv_a,
-                6,
-                1 + odd,
-                n,
-                (lax.rem(c + 2 - odd, BLOCKS), 2 * flip(p, far) + jnp.where(odd == 1, k, 1)),
-            ),
-        )
-
-    def in_relay(n):
-        return remote(
-            lead.at[n, 4],
-            lead.at[n, 3 - k - 2 * cross[-1]],
+        )
+
+    def in_core(n):
+        return remote(own.at[n, 2], own.at[n, 3], send_a, recv_a, 4, 1, n, other_core)
+
+    def in_one(n, far):
+        chip = flip(p, cross[1])
+        return remote(
+            own.at[n, 2 * flip(far, cross[1]), chip],
+            lead.at[n, k + 2 * far],
             send_a,
             recv_a,
-            7,
-            1,
+            2 + far,
+            2 - far,
+            n,
+            (block(1), 2 * chip),
+        )
+
+    def in_two(n, far):
+        chip = flip(p, cross[2])
+        direct = z == 1
+        step = jnp.where(direct, 2, jnp.where(z == 0, 3, -1))
+        device = jnp.where(direct, 2 * chip + 1, g)
+        return remote(
+            own.at[n, 2 * flip(far, cross[2]), chip],
+            lead.at[n, jnp.where(direct, 1 - k + 2 * far, 4 + far)],
+            send_a,
+            recv_a,
+            5 + far,
+            jnp.where(direct, 2 - far, 3 + far),
+            n,
+            (block(step), device),
+        )
+
+    in_between = z != 0
+
+    def in_pass(n, far):
+        chip = flip(p, flag((spot == HALF_RING - 3) | (spot == HALF_RING - 2)))
+        return remote(
+            lead.at[n, 4 + far],
+            lead.at[n, 1 - k + 2 * far],
+            send_a,
+            recv_a,
+            7 + far,
+            2 - far,
+            n,
+            (block(jnp.where(z == 3, -1, 3)), 2 * chip + 1),
+        )
+
+    def in_share(n, slot):
+        return remote(
+            lead.at[n, slot],
+            lead.at[n, 1 - slot],
+            send_a,
+            recv_a,
+            9 + slot,
+            2,
             n,
             (block(1), 2 * p + 1),
         )
+
+    def in_leads(n, second):
+        in_one(n, flip(second, cross[1])).start()
+        far = flip(second, cross[2])
+
+        @pl.when((far == 1) | ((k == 1) & jnp.logical_not(third(n))))
+        def _():
+            in_two(n, far).start()
 
     def sent(ref, sends, kind):
         pltpu.make_async_remote_copy(
@@ -258,29 +275,55 @@
         @pl.when(n < CHUNKS)
         def _():
             own[n, 0] = stage[n].astype(BF)
-            for copy in in_first(n):
+            for copy in in_bands(n):
                 copy.start()
+            in_leads(n, 0)
             make_factor(n)
 
-        @pl.when((n >= 1) & (n < CHUNKS + 1))
-        def _():
-            arrived_a(own.at[n - 1, 2], 0, n - 1)
-            for copy in in_second(n - 1):
-                copy.start()
-
-        @pl.when((n >= 2) & (n < CHUNKS + 2) & (odd == 0))
-        def _():
-            arrived_a(lead.at[n - 2, 4], 2, n - 2)
-            in_relay(n - 2).start()
-
-        @pl.when(n >= 3)
-        def _():
-            arrived_a(own.at[n - 3], 1, n - 3)
-            forward(n - 3)
+        @pl.when((n >= IN_LAGS[0]) & (n < CHUNKS + IN_LAGS[0]))
+        def _():
+            m = n - IN_LAGS[0]
+            arrived_a(own.at[m, 2], 0, m)
+            in_leads(m, 1)
+            in_core(m).start()
+
+        @pl.when((n >= IN_LAGS[1]) & (n < CHUNKS + IN_LAGS[1]))
+        def _():
+            m = n - IN_LAGS[1]
+
+            @pl.when(in_between)
+            def _():
+                arrived_a(lead.at[m, 5], 4, m)
+                in_pass(m, 1).start()
+
+                @pl.when((k == 1) & jnp.logical_not(third(m)))
+                def _():
+                    arrived_a(lead.at[m, 4], 3, m)
+                    in_pass(m, 0).start()
+
+            @pl.when(k == 0)
+            def _():
+                arrived_a(lead.at[m, 0:2], 2, m)
+                in_share(m, 0).start()
+
+                @pl.when(third(m))
+                def _():
+                    in_share(m, 1).start()
+
+        @pl.when(n >= IN_LAGS[2])
+        def _():
+            m = n - IN_LAGS[2]
+
+            @pl.when(k == 1)
+            def _():
+                arrived_a(lead.at[m, 0:2], 2, m)
+
+            arrived_a(own.at[m, 0:3], 1, m)
+            forward(m)
 
         return carry
 
-    lax.fori_loop(0, CHUNKS + 3, in_step, 0)
+    lax.fori_loop(0, CHUNKS + IN_LAGS[2], in_step, 0)
 
     def middle(step):
         for t in (4 * step + i for i in range(4)):
@@ -302,23 +345,33 @@
 
     each(TILES // 4, middle)
 
-    for kind, ref in enumerate(
-        (own.at[:, 0],) * 2 + (own.at[:, 0, 0],) * 2 + (own.at[:, 2],) + (own.at[:, 2, 0],) * 2
-    ):
+    one, some, rest = lead.at[:, 0], lead.at[:THIRDS, 0], lead.at[THIRDS:, 0]
+    for kind, ref in enumerate((own.at[:, 0], own.at[:, 0], one, one, own.at[:, 2])):
         sent(ref, send_a, kind)
-
-    @pl.when(odd == 0)
+    sent(one, send_a, 6)
+
+    @pl.when(k == 1)
     def _():
-        sent(lead.at[:, 4], send_a, 7)
+        sent(rest, send_a, 5)
+
+    @pl.when(k == 0)
+    def _():
+        sent(one, send_a, 9)
+        sent(some, send_a, 10)
+
+    @pl.when(in_between)
+    def _():
+        sent(one, send_a, 8)
+
+        @pl.when(k == 1)
+        def _():
+            sent(rest, send_a, 7)
 
     note.wait()
-    weights = []
-    for j in range(2):
-        kept = jnp.where(k == 0, note_in[1 + j : 2 + j, :], keep[j, 1, p].astype(F32))
-        for amount in (occ[j], note_in[0:1, :]):
-            row = -(amount * kept)
-            weights.append(jnp.concatenate([row, row], 1))
-    own0, lead0, own1, lead1 = weights
+    kept = [keep[j, k, p].astype(F32) for j in range(2)]
+    own0, own1 = (-(occ[j] * kept[j]) for j in range(2))
+    amount = jnp.concatenate([note_in[0:1, :]] * 2, 1)
+    lead0, lead1 = (-(amount * kept[j]) for j in range(2))
 
     def inverse(n):
         for pair in range(PAIRS):
@@ -347,104 +400,188 @@
                 own[n, s, 0, :, lanes] = ((lead0 * x0) * a).astype(BF)
                 own[n, s, 1, :, lanes] = ((lead1 * x1) * a).astype(BF)
 
-    home = lax.rem(c + BLOCKS + 1 - 3 * k, BLOCKS)
-    home_cross = jnp.where(k == 0, cross[1], cross[-2])
-    hop = k * (1 - odd)
-
-    def out_first(n):
-        chip = 2 * flip(p, home_cross)
-
-        def lead_out(slot, core):
-            away = slot // 2
-            hands_on = flip(away, home_cross)
-            relayed = away * hop
-            kind = k + 2 * hands_on + relayed * (4 - k - 2 * hands_on)
-            device = (lax.rem(home + relayed, BLOCKS), chip + core)
-            sort = (1 - hands_on) * (1 - relayed) + 2 * relayed
-            return remote(
-                lead.at[n, slot], sums_in.at[n, kind], send_b, recv_b, 2 + slot, sort, n, device
-            )
-
+    def out_core(n):
         return (
             remote(own.at[n, 1], core_in.at[n, 0], send_b, recv_b, 0, 1, n, other_core),
             remote(own.at[n, 3], core_in.at[n, 1], send_b, recv_b, 1, 0, n, other_core),
-            lead_out(0, k),
-            lead_out(1, 1 - k),
-            lead_out(2, k),
-            lead_out(3, 1 - k),
-        )
-
-    def out_relay(n):
-        return remote(
-            sums_in.at[n, 4],
-            sums_in.at[n, 3 - 2 * cross[1]],
+        )
+
+    def out_one(n, slot):
+        far = slot // 2
+        return remote(
+            lead.at[n, slot],
+            sums_in.at[n, far],
             send_b,
             recv_b,
-            6,
-            cross[1],
-            n,
-            (block(-1), g),
+            2 + slot,
+            1 - flip(far, cross[-1]),
+            n,
+            (block(-1), 2 * flip(p, cross[-1]) + slot % 2),
+        )
+
+    def out_two(n, slot):
+        far = slot // 2
+        core = 1 - slot % 2
+        direct = z == 2
+        step = jnp.where(direct, -2, jnp.where(z == 3, -3, 1))
+        chip = jnp.where(direct, flip(p, cross[-2]), p)
+        index = far + jnp.where(direct, 2, 4)
+        return remote(
+            lead.at[n, slot],
+            sums_in.at[n, index],
+            send_b,
+            recv_b,
+            2 + slot,
+            index,
+            n,
+            (block(step), 2 * chip + core),
+        )
+
+    out_between = z != 3
+
+    def out_pass(n, far):
+        chip = flip(p, flag((spot == 1) | (spot == 2)))
+        return remote(
+            sums_in.at[n, 4 + far],
+            sums_in.at[n, 2 + far],
+            send_b,
+            recv_b,
+            6 + far,
+            2 + far,
+            n,
+            (block(jnp.where(z == 0, 1, -3)), 2 * chip + k),
+        )
+
+    def out_share(n, slot):
+        return remote(
+            lead.at[n, slot],
+            sums_in.at[n, 7 - slot],
+            send_b,
+            recv_b,
+            2 + slot,
+            4 - 2 * slot,
+            n,
+            (block(-1), 2 * p),
         )
 
     def out_chip(n):
-        return remote(own.at[n, 2], chip_in.at[n], send_b, recv_b, 7, 3, n, other_chip)
+        return remote(own.at[n, 2], chip_in.at[n], send_b, recv_b, 8, 6, n, other_chip)
 
     def arrived_b(ref, sort, n):
         remote(ref, ref, send_b, recv_b, 0, sort, n, other_core).wait_recv()
 
-    bands = [flip(p, cross[-1]), flip(p, cross[2])]
+    bands = [flip(p, cross[1]), flip(p, cross[2])]
     masks = [[flag(b == band).astype(F32) for b in bands] for band in range(2)]
 
-    def lead_sums(m, first, band):
-        return masks[band][0] * sums_in[m, first].astype(F32) + masks[band][1] * sums_in[
-            m, first + 1
-        ].astype(F32)
+    def lead_sums(m, far, band):
+        first = sums_in[m, flip(far, cross[1])].astype(F32)
+        second = sums_in[m, 2 + flip(far, cross[2])].astype(F32)
+        return masks[band][0] * first + masks[band][1] * second
 
     def out_step(n, carry):
         @pl.when(n < CHUNKS)
         def _():
             inverse(n)
-            for copy in out_first(n):
+
+            @pl.when(k == 0)
+            def _():
+                out_one(n, 2).start()
+                out_one(n, 3).start()
+
+                @pl.when(jnp.logical_not(third(n)))
+                def _():
+                    out_one(n, 1).start()
+
+            @pl.when(k == 1)
+            def _():
+                out_share(n, 1).start()
+                out_two(n, 2).start()
+                out_two(n, 3).start()
+
+                @pl.when(third(n))
+                def _():
+                    out_share(n, 0).start()
+
+                @pl.when(jnp.logical_not(third(n)))
+                def _():
+                    out_two(n, 0).start()
+
+            for copy in out_core(n):
                 copy.start()
 
-        @pl.when((n >= 1) & (n < CHUNKS + 1) & (odd == 1))
-        def _():
-            arrived_b(sums_in.at[n - 1, 4], 2, n - 1)
-            out_relay(n - 1).start()
-
-        @pl.when((n >= 2) & (n < CHUNKS + 2))
-        def _():
-            m = n - 2
-            arrived_b(core_in.at[m], 0, m)
+        @pl.when((n >= OUT_LAGS[0]) & (n < CHUNKS + OUT_LAGS[0]))
+        def _():
+            m = n - OUT_LAGS[0]
+
+            @pl.when(out_between)
+            def _():
+                arrived_b(sums_in.at[m, 5], 5, m)
+                out_pass(m, 1).start()
+
+                @pl.when((k == 1) & jnp.logical_not(third(m)))
+                def _():
+                    arrived_b(sums_in.at[m, 4], 4, m)
+                    out_pass(m, 0).start()
+
+        @pl.when((n >= OUT_LAGS[1]) & (n < CHUNKS + OUT_LAGS[1]))
+        def _():
+            m = n - OUT_LAGS[1]
+
+            @pl.when(k == 0)
+            def _():
+                arrived_b(sums_in.at[m, 6], 2, m)
+                total = lead[m, 0].astype(F32) + sums_in[m, 6].astype(F32)
+                lead[m, 0] = total.astype(BF)
+                out_one(m, 0).start()
+
+                @pl.when(third(m))
+                def _():
+                    arrived_b(sums_in.at[m, 7], 4, m)
+                    total = lead[m, 1].astype(F32) + sums_in[m, 7].astype(F32)
+                    lead[m, 1] = total.astype(BF)
+                    out_one(m, 1).start()
+
+        @pl.when((n >= OUT_LAGS[2]) & (n < CHUNKS + OUT_LAGS[2]))
+        def _():
+            m = n - OUT_LAGS[2]
+            arrived_b(own.at[m, 0:3, 0], 0, m)
+            arrived_b(sums_in.at[m, 3], 3, m)
+
+            @pl.when((k == 1) & jnp.logical_not(third(m)))
+            def _():
+                arrived_b(sums_in.at[m, 2], 2, m)
+
             for band in range(2):
                 total = own[m, 2, band].astype(F32) + core_in[m, 1, band].astype(F32)
-                own[m, 2, band] = (total + lead_sums(m, 2, band)).astype(BF)
+                own[m, 2, band] = (total + lead_sums(m, 1, band)).astype(BF)
             out_chip(m).start()
 
-        @pl.when(n >= 4)
-        def _():
-            m = n - 4
-            arrived_b(core_in.at[m], 1, m)
-            arrived_b(chip_in.at[m], 3, m)
+        @pl.when(n >= OUT_LAGS[3])
+        def _():
+            m = n - OUT_LAGS[3]
+            arrived_b(own.at[m, 0:3, 0], 1, m)
+            arrived_b(chip_in.at[m], 6, m)
             for band in range(2):
                 total = own[m, 0, band].astype(F32) + core_in[m, 0, band].astype(F32)
-                stage[m, band] = (
-                    total + chip_in[m, band].astype(F32) + lead_sums(m, 0, band)
-                )
+                stage[m, band] = total + chip_in[m, band].astype(F32) + lead_sums(m, 0, band)
             store(m).start()
 
         return carry
 
-    lax.fori_loop(0, CHUNKS + 4, out_step, 0)
-
-    for kind, ref in enumerate((own.at[:, 0],) * 2 + (lead.at[:, 0],) * 4):
+    lax.fori_loop(0, CHUNKS + OUT_LAGS[3], out_step, 0)
+
+    for kind, ref in enumerate((own.at[:, 0],) * 2 + (one,) * 4):
         sent(ref, send_b, kind)
 
-    @pl.when(odd == 1)
+    @pl.when(out_between)
     def _():
-        sent(sums_in.at[:, 4], send_b, 6)
-
-    sent(own.at[:, 2], send_b, 7)
+        sent(one, send_b, 7)
+
+        @pl.when(k == 1)
+        def _():
+            sent(rest, send_b, 6)
+
+    sent(own.at[:, 2], send_b, 8)
     pltpu.make_async_copy(stage, stage, store_sem.at[0]).wait()
 
 
@@ -461,26 +598,26 @@
         out_specs=anywhere,
         scratch_shapes=[
             pltpu.VMEM((CHUNKS, 2, SLAB, LANES), F32),
-            pltpu.VMEM((CHUNKS, 5, SLAB, LANES), BF),
+            pltpu.VMEM((CHUNKS, 6, SLAB, LANES), BF),
             pltpu.VMEM((CHUNKS, 4, 2, SLAB, LANES), BF),
             pltpu.VMEM((TILES, 8 * GRID, GRID), F32),
             pltpu.VMEM((TILES, 8 * GRID, GRID), F32),
             pltpu.VMEM((GRID, GRID, GRID), F32),
-            pltpu.VMEM((CHUNKS, 5, SLAB, LANES), BF),
+            pltpu.VMEM((CHUNKS, 8, SLAB, LANES), BF),
             pltpu.VMEM((CHUNKS, 2, 2, SLAB, LANES), BF),
             pltpu.VMEM((CHUNKS, 2, SLAB, LANES), BF),
             pltpu.VMEM((8, GRID), F32),
             pltpu.VMEM((8, GRID), F32),
             dma((1,)),
             dma((1,)),
-            dma((8,)),
-            dma((3, CHUNKS)),
-            dma((8,)),
-            dma((4, CHUNKS)),
+            dma((11,)),
+            dma((5, CHUNKS)),
+            dma((9,)),
+            dma((7, CHUNKS)),
             dma((2,)),
         ],
         compiler_params=pltpu.CompilerParams(
-            collective_id=0, has_side_effects=True, vmem_limit_bytes=60 * 1024 * 1024
+            collective_id=0, has_side_effects=True, vmem_limit_bytes=62 * 1024 * 1024
         ),
         name="exchange",
     )(occupation, pair_keep, orbitals, jnp.asarray(plus), jnp.asarray(minus))

time: 178 us -> 165 us (0.927)
  Pallas kernels: 172 us -> 159 us
    pallas_call x1, Pallas kernels: 172 us -> 159 us  [body(): pl.pallas_call(kernel, out_shape=jax.ShapeDtypeStruct(orbitals.shape, F32...]
where the time goes in v5:
time: 165 us; the launch traced here: 164 us
  Pallas kernels  159 us (96%)
  local copies, waits for them, and re-layouts  4.5 us (3%)
    pallas_call x1, Pallas kernels, body(): pl.pallas_call(kernel, out_shape=jax.ShapeDtypeStruct(orbitals.shape, F32...  159 us
    unnamed x1, local copies, waits for them, and re-layouts  4.5 us

profile of v5, /device:TPU:8, one launch (start us, length us, event | category | flops | bytes accessed | tf_op | source)
XLA Modules:
  0.0 163.7 jit_solution(15506828618348065269)
XLA Ops:
  0.0 159.2 %exchange.1 = f32[2,32,16384]{2,1,0:T(8,128)} custom-call(f32[2]{0:T(128)} %occ.1, s32[2,2,2]{2,1,0:T(2,128)} %keep.1, f32[2,32,16384]{2,1,0:T(8,128)} %orbitals.1, bf16[256,256]{1,0:T(8,128)(2,1)} %constant.4.clone.plus, bf16[256,256]{1,0:T(8,128)(2,1)} %constant.5.clone.minus), custom_call_target="tpu_custom_call" | custom-call | tf_op jit(solution)/shard_map/exchange/pallas_call | solution.py:594
  159.2 4.5 %copy.7 = f32[2,32,16384]{2,1,0:T(8,128)} copy(f32[2,32,16384]{2,1,0:T(8,128)} %exchange.1) | data formatting | bytes 8388608

commit v6 on v5

--- a/solution.py
+++ b/solution.py
@@ -18,8 +18,8 @@
 LANES = GRID * GRID // CHUNKS
 PAIRS = LANES // (2 * GRID)
 TILES = GRID // 8
-IN_LAGS = (2, 4, 8)
-OUT_LAGS = (2, 2, 3, 5)
+IN_LAGS = (3, 5, 9)
+OUT_LAGS = (3, 3, 4, 6)
 THIRDS = sum(n % 3 == 2 for n in range(CHUNKS))
 BF = jnp.bfloat16
 F32 = jnp.float32
@@ -47,8 +47,8 @@
 
 def kernel(
     occ, keep, orbitals, plus, minus, out,
-    stage, lead, own, real, imag, factor, sums_in, core_in, chip_in, note_out, note_in,
-    load_sem, store_sem, send_a, recv_a, send_b, recv_b, note_sem,
+    lead, own, real, imag, factor, sums_in, core_in, chip_in, note_out, note_in,
+    load_sem, send_a, recv_a, send_b, recv_b, note_sem,
 ):
     c, g = lax.axis_index("band"), lax.axis_index("grid")
     p, k = lax.div(g, 2), lax.rem(g, 2)
@@ -85,13 +85,11 @@
     other_core = (c, 2 * p + 1 - k)
     other_chip = (c, 2 * (1 - p) + k)
 
-    def load(n):
-        lanes = pl.ds(pl.multiple_of(n * LANES, LANES), LANES)
-        return pltpu.make_async_copy(orbitals.at[:, :, lanes], stage.at[n], load_sem.at[0])
-
-    def store(n):
-        lanes = pl.ds(pl.multiple_of(n * LANES, LANES), LANES)
-        return pltpu.make_async_copy(stage.at[n], out.at[:, :, lanes], store_sem.at[0])
+    def part(n):
+        return pl.ds(pl.multiple_of(n * LANES, LANES), LANES)
+
+    def third(n):
+        return lax.rem(n, 3) == 2
 
     def each(count, step):
         def run(n, carry):
@@ -100,33 +98,38 @@
 
         lax.fori_loop(0, count, run, 0)
 
-    each(CHUNKS, lambda n: load(n).start())
-
-    def clear(n):
-        @pl.when((k == 0) | (lax.rem(n, 3) == 2))
-        def _():
-            sums_in[n, 2] = jnp.zeros((SLAB, LANES), BF)
-
-    each(CHUNKS, clear)
-
     barrier = pltpu.get_barrier_semaphore()
 
     def greet(band, grid):
         pl.semaphore_signal(barrier, inc=1, device_id=(band, grid), device_id_type=MESH)
 
-    for away in (1, 2, 3):
-        greet(c, lax.rem(g + away, 4))
-    for step in cross:
+    for step in (1, -1):
+
+        @pl.when(cross[step] == 1)
+        def _(step=step):
+            for core in (0, 1):
+                greet(block(step), 2 * (1 - p) + core)
+
+    for step in (3, -3, 1, -1, 2, -2):
         for core in (0, 1):
-            greet(block(step), 2 * p + core)
-
-            @pl.when(cross[step] == 1)
-            def _(step=step, core=core):
-                greet(block(step), 2 * (1 - p) + core)
-
-    pl.semaphore_wait(barrier, 15 + 2 * sum(cross.values()))
-
+            greet(block(step), 2 * (flip(p, cross[step]) if abs(step) == 3 else p) + core)
+    greet(*other_core)
+    greet(*other_chip)
+
+    fetch = pltpu.make_async_copy(orbitals, out, load_sem.at[0])
+    fetch.start()
+
+    def clear(n):
+        @pl.when((k == 0) | third(n))
+        def _():
+            sums_in[n, 2] = jnp.zeros((SLAB, LANES), BF)
+
+    each(CHUNKS, clear)
     note_out[...] = jnp.zeros((8, GRID), F32) + occ[p]
+    fetch.wait()
+    own[0, 0] = out[:, :, part(0)].astype(BF)
+    pl.semaphore_wait(barrier, 14 + 2 * (cross[1] + cross[-1]))
+
     note = pltpu.make_async_remote_copy(
         src_ref=note_out,
         dst_ref=note_in,
@@ -136,9 +139,6 @@
         device_id_type=MESH,
     )
     note.start()
-
-    def third(n):
-        return lax.rem(n, 3) == 2
 
     def in_bands(n):
         mine = own.at[n, 0]
@@ -269,15 +269,18 @@
                     real[t, rows, :] = result[at : at + 8, :GRID]
                     imag[t, rows, :] = result[at : at + 8, GRID:]
 
-    pltpu.make_async_copy(stage, stage, load_sem.at[0]).wait()
-
     def in_step(n, carry):
         @pl.when(n < CHUNKS)
         def _():
-            own[n, 0] = stage[n].astype(BF)
             for copy in in_bands(n):
                 copy.start()
             in_leads(n, 0)
+            later = jnp.minimum(n + 1, CHUNKS - 1)
+
+            @pl.when(later > n)
+            def _():
+                own[later, 0] = out[:, :, part(later)].astype(BF)
+
             make_factor(n)
 
         @pl.when((n >= IN_LAGS[0]) & (n < CHUNKS + IN_LAGS[0]))
@@ -326,7 +329,7 @@
     lax.fori_loop(0, CHUNKS + IN_LAGS[2], in_step, 0)
 
     def middle(step):
-        for t in (4 * step + i for i in range(4)):
+        for t in (8 * step + i for i in range(8)):
             for pair in range(4):
                 pick = [pl.ds(2 * pair + half, GRID, stride=8) for half in range(2)]
                 packed = jnp.concatenate(
@@ -343,7 +346,7 @@
                     real[t, pick[half], :] = result[:GRID, at]
                     imag[t, pick[half], :] = result[GRID:, at]
 
-    each(TILES // 4, middle)
+    each(TILES // 8, middle)
 
     one, some, rest = lead.at[:, 0], lead.at[:THIRDS, 0], lead.at[THIRDS:, 0]
     for kind, ref in enumerate((own.at[:, 0], own.at[:, 0], one, one, own.at[:, 2])):
@@ -563,8 +566,9 @@
             arrived_b(chip_in.at[m], 6, m)
             for band in range(2):
                 total = own[m, 0, band].astype(F32) + core_in[m, 0, band].astype(F32)
-                stage[m, band] = total + chip_in[m, band].astype(F32) + lead_sums(m, 0, band)
-            store(m).start()
+                out[band, :, part(m)] = (
+                    total + chip_in[m, band].astype(F32) + lead_sums(m, 0, band)
+                )
 
         return carry
 
@@ -582,7 +586,6 @@
             sent(rest, send_b, 6)
 
     sent(own.at[:, 2], send_b, 8)
-    pltpu.make_async_copy(stage, stage, store_sem.at[0]).wait()
 
 
 def body(orbitals, occupation, pair_keep):
@@ -593,11 +596,10 @@
     dma = pltpu.SemaphoreType.DMA
     return pl.pallas_call(
         kernel,
-        out_shape=jax.ShapeDtypeStruct(orbitals.shape, F32),
+        out_shape=pltpu.VMEM(orbitals.shape, F32),
         in_specs=[smem, smem, anywhere, vmem, vmem],
-        out_specs=anywhere,
+        out_specs=vmem,
         scratch_shapes=[
-            pltpu.VMEM((CHUNKS, 2, SLAB, LANES), F32),
             pltpu.VMEM((CHUNKS, 6, SLAB, LANES), BF),
             pltpu.VMEM((CHUNKS, 4, 2, SLAB, LANES), BF),
             pltpu.VMEM((TILES, 8 * GRID, GRID), F32),
@@ -609,7 +611,6 @@
             pltpu.VMEM((8, GRID), F32),
             pltpu.VMEM((8, GRID), F32),
             dma((1,)),
-            dma((1,)),
             dma((11,)),
             dma((5, CHUNKS)),
             dma((9,)),
@@ -617,7 +618,7 @@
             dma((2,)),
         ],
         compiler_params=pltpu.CompilerParams(
-            collective_id=0, has_side_effects=True, vmem_limit_bytes=62 * 1024 * 1024
+            collective_id=0, has_side_effects=True, vmem_limit_bytes=58 * 1024 * 1024
         ),
         name="exchange",
     )(occupation, pair_keep, orbitals, jnp.asarray(plus), jnp.asarray(minus))

time: 165 us -> 160 us (0.970)
  Pallas kernels: 159 us -> 156 us
  local copies, waits for them, and re-layouts: 4.5 us -> 2.02 us
    pallas_call x1, Pallas kernels: 159 us -> 156 us  [body(): pl.pallas_call(kernel, out_shape=pltpu.VMEM(orbitals.shape, F32), in_spec...]
    unnamed x1, local copies, waits for them, and re-layouts: 4.5 us -> 2.02 us
where the time goes in v6:
time: 160 us; the launch traced here: 158 us
  Pallas kernels  156 us (98%)
  local copies, waits for them, and re-layouts  2.02 us (1%)
    pallas_call x1, Pallas kernels, body(): pl.pallas_call(kernel, out_shape=pltpu.VMEM(orbitals.shape, F32), in_spec...  156 us

profile of v6, /device:TPU:8, one launch (start us, length us, event | category | flops | bytes accessed | tf_op | source)
XLA Modules:
  0.0 158.4 jit_solution(11940334941779889083)
XLA Ops:
  0.0 156.4 %exchange.1 = f32[2,32,16384]{2,1,0:T(8,128)S(1)} custom-call(f32[2]{0:T(128)} %occ.1, s32[2,2,2]{2,1,0:T(2,128)} %keep.1, f32[2,32,16384]{2,1,0:T(8,128)} %orbitals.1, bf16[256,256]{1,0:T(8,128)(2,1)} %constant.4.clone.plus, bf16[256,256]{1,0:T(8,128)(2,1)} %constant.5.clone.minus), custom_call_target="tpu_custom_call" | custom-call | tf_op jit(solution)/shard_map/exchange/pallas_call | solution.py:597
  156.4 2.0 %copy.7 = f32[2,32,16384]{2,1,0:T(8,128)} copy(f32[2,32,16384]{2,1,0:T(8,128)S(1)} %exchange.1) | data formatting | bytes 8388608

commit v7 on v6

--- a/solution.py
+++ b/solution.py
@@ -18,9 +18,9 @@
 LANES = GRID * GRID // CHUNKS
 PAIRS = LANES // (2 * GRID)
 TILES = GRID // 8
-IN_LAGS = (3, 5, 9)
+IN_LAGS = (4, 6, 10)
 OUT_LAGS = (3, 3, 4, 6)
-THIRDS = sum(n % 3 == 2 for n in range(CHUNKS))
+THIRDS = CHUNKS // 3
 BF = jnp.bfloat16
 F32 = jnp.float32
 MESH = pl.DeviceIdType.MESH
@@ -89,7 +89,7 @@
         return pl.ds(pl.multiple_of(n * LANES, LANES), LANES)
 
     def third(n):
-        return lax.rem(n, 3) == 2
+        return (lax.rem(n, 2) == 0) & (n < 2 * THIRDS)
 
     def each(count, step):
         def run(n, carry):
@@ -174,7 +174,7 @@
             send_a,
             recv_a,
             5 + far,
-            jnp.where(direct, 2 - far, 3 + far),
+            jnp.where(direct, 2 - far, 3),
             n,
             (block(step), device),
         )
@@ -296,13 +296,18 @@
 
             @pl.when(in_between)
             def _():
-                arrived_a(lead.at[m, 5], 4, m)
+                both = (k == 1) & jnp.logical_not(third(m))
+
+                @pl.when(both)
+                def _():
+                    arrived_a(lead.at[m, 4:6], 3, m)
+                    in_pass(m, 0).start()
+
+                @pl.when(jnp.logical_not(both))
+                def _():
+                    arrived_a(lead.at[m, 5], 3, m)
+
                 in_pass(m, 1).start()
-
-                @pl.when((k == 1) & jnp.logical_not(third(m)))
-                def _():
-                    arrived_a(lead.at[m, 4], 3, m)
-                    in_pass(m, 0).start()
 
             @pl.when(k == 0)
             def _():
@@ -435,7 +440,7 @@
             send_b,
             recv_b,
             2 + slot,
-            index,
+            jnp.where(direct, 2 - 2 * far, 3 + far),
             n,
             (block(step), 2 * chip + core),
         )
@@ -450,7 +455,7 @@
             send_b,
             recv_b,
             6 + far,
-            2 + far,
+            2 - 2 * far,
             n,
             (block(jnp.where(z == 0, 1, -3)), 2 * chip + k),
         )
@@ -462,13 +467,13 @@
             send_b,
             recv_b,
             2 + slot,
-            4 - 2 * slot,
+            3 - slot,
             n,
             (block(-1), 2 * p),
         )
 
     def out_chip(n):
-        return remote(own.at[n, 2], chip_in.at[n], send_b, recv_b, 8, 6, n, other_chip)
+        return remote(own.at[n, 2], chip_in.at[n], send_b, recv_b, 8, 1, n, other_chip)
 
     def arrived_b(ref, sort, n):
         remote(ref, ref, send_b, recv_b, 0, sort, n, other_core).wait_recv()
@@ -518,12 +523,12 @@
 
             @pl.when(out_between)
             def _():
-                arrived_b(sums_in.at[m, 5], 5, m)
+                arrived_b(sums_in.at[m, 5], 4, m)
                 out_pass(m, 1).start()
 
                 @pl.when((k == 1) & jnp.logical_not(third(m)))
                 def _():
-                    arrived_b(sums_in.at[m, 4], 4, m)
+                    arrived_b(sums_in.at[m, 4], 3, m)
                     out_pass(m, 0).start()
 
         @pl.when((n >= OUT_LAGS[1]) & (n < CHUNKS + OUT_LAGS[1]))
@@ -539,7 +544,7 @@
 
                 @pl.when(third(m))
                 def _():
-                    arrived_b(sums_in.at[m, 7], 4, m)
+                    arrived_b(sums_in.at[m, 7], 3, m)
                     total = lead[m, 1].astype(F32) + sums_in[m, 7].astype(F32)
                     lead[m, 1] = total.astype(BF)
                     out_one(m, 1).start()
@@ -547,8 +552,7 @@
         @pl.when((n >= OUT_LAGS[2]) & (n < CHUNKS + OUT_LAGS[2]))
         def _():
             m = n - OUT_LAGS[2]
-            arrived_b(own.at[m, 0:3, 0], 0, m)
-            arrived_b(sums_in.at[m, 3], 3, m)
+            arrived_b(sums_in.at[m, 0:4], 0, m)
 
             @pl.when((k == 1) & jnp.logical_not(third(m)))
             def _():
@@ -562,8 +566,7 @@
         @pl.when(n >= OUT_LAGS[3])
         def _():
             m = n - OUT_LAGS[3]
-            arrived_b(own.at[m, 0:3, 0], 1, m)
-            arrived_b(chip_in.at[m], 6, m)
+            arrived_b(sums_in.at[m, 0:5], 1, m)
             for band in range(2):
                 total = own[m, 0, band].astype(F32) + core_in[m, 0, band].astype(F32)
                 out[band, :, part(m)] = (
@@ -612,9 +615,9 @@
             pltpu.VMEM((8, GRID), F32),
             dma((1,)),
             dma((11,)),
+            dma((4, CHUNKS)),
+            dma((9,)),
             dma((5, CHUNKS)),
-            dma((9,)),
-            dma((7, CHUNKS)),
             dma((2,)),
         ],
         compiler_params=pltpu.CompilerParams(

time: 160 us -> 159 us (level)
  no operation moved by 1% of the time
where the time goes in v7:
time: 159 us
  Pallas kernels  157 us (99%)
  local copies, waits for them, and re-layouts  2.02 us (1%)
    pallas_call x1, Pallas kernels, body(): pl.pallas_call(kernel, out_shape=pltpu.VMEM(orbitals.shape, F32), in_spec...  157 us

profile of v7, /device:TPU:8, one launch (start us, length us, event | category | flops | bytes accessed | tf_op | source)
XLA Modules:
  0.0 158.8 jit_solution(13806301468949820023)
XLA Ops:
  0.0 156.8 %exchange.1 = f32[2,32,16384]{2,1,0:T(8,128)S(1)} custom-call(f32[2]{0:T(128)} %occ.1, s32[2,2,2]{2,1,0:T(2,128)} %keep.1, f32[2,32,16384]{2,1,0:T(8,128)} %orbitals.1, bf16[256,256]{1,0:T(8,128)(2,1)} %constant.4.clone.plus, bf16[256,256]{1,0:T(8,128)(2,1)} %constant.5.clone.minus), custom_call_target="tpu_custom_call" | custom-call | tf_op jit(solution)/shard_map/exchange/pallas_call | solution.py:600
  156.8 2.0 %copy.7 = f32[2,32,16384]{2,1,0:T(8,128)} copy(f32[2,32,16384]{2,1,0:T(8,128)S(1)} %exchange.1) | data formatting | bytes 8388608

commit v8 on v7

--- a/solution.py
+++ b/solution.py
@@ -605,8 +605,8 @@
         scratch_shapes=[
             pltpu.VMEM((CHUNKS, 6, SLAB, LANES), BF),
             pltpu.VMEM((CHUNKS, 4, 2, SLAB, LANES), BF),
-            pltpu.VMEM((TILES, 8 * GRID, GRID), F32),
-            pltpu.VMEM((TILES, 8 * GRID, GRID), F32),
+            pltpu.VMEM((TILES, 8 * GRID + 8, GRID), F32),
+            pltpu.VMEM((TILES, 8 * GRID + 8, GRID), F32),
             pltpu.VMEM((GRID, GRID, GRID), F32),
             pltpu.VMEM((CHUNKS, 8, SLAB, LANES), BF),
             pltpu.VMEM((CHUNKS, 2, 2, SLAB, LANES), BF),

time: 159 us -> 159 us (level)
  no operation moved by 1% of the time
where the time goes in v8:
time: 159 us
  Pallas kernels  157 us (99%)
  local copies, waits for them, and re-layouts  2.02 us (1%)
    pallas_call x1, Pallas kernels, body(): pl.pallas_call(kernel, out_shape=pltpu.VMEM(orbitals.shape, F32), in_spec...  157 us

profile of v8, /device:TPU:8, one launch (start us, length us, event | category | flops | bytes accessed | tf_op | source)
XLA Modules:
  0.0 158.8 jit_solution(14845696077996906824)
XLA Ops:
  0.0 156.7 %exchange.1 = f32[2,32,16384]{2,1,0:T(8,128)S(1)} custom-call(f32[2]{0:T(128)} %occ.1, s32[2,2,2]{2,1,0:T(2,128)} %keep.1, f32[2,32,16384]{2,1,0:T(8,128)} %orbitals.1, bf16[256,256]{1,0:T(8,128)(2,1)} %constant.4.clone.plus, bf16[256,256]{1,0:T(8,128)(2,1)} %constant.5.clone.minus), custom_call_target="tpu_custom_call" | custom-call | tf_op jit(solution)/shard_map/exchange/pallas_call | solution.py:600
  156.8 2.0 %copy.7 = f32[2,32,16384]{2,1,0:T(8,128)} copy(f32[2,32,16384]{2,1,0:T(8,128)S(1)} %exchange.1) | data formatting | bytes 8388608
